TPU v7x, 32 devices: a whole 2x2x4 slice. The times are simulated.
32 devices in a mesh: rx: 8 (over z, core), ry: 4 (over y, x).
Axes of the slice: x: 2, y: 2, z: 4, core: 2. Of those that a mesh axis runs over, the one named last changes fastest.
Arguments:
- primal: bfloat16 [4096, 320], P(('rx', 'ry')), may hold values from -6 to 6
- adjoint: bfloat16 [4096, 320], P(('rx', 'ry')), may hold values from -6 to 6
- send_index: int32 [128, 16], P(('rx', 'ry')), may hold values from 0 to 127, as said below
- neighbours: int32 [4096, 6], P(('rx', 'ry')), may hold values from 0 to 191, as said below
- recon: bfloat16 [7, 64, 125], replicated, may hold values from -0.25 to 0.25
- deriv: bfloat16 [3, 125, 125], replicated, may hold values from -0.5 to 0.5
- jacob: float32 [3, 5, 5], replicated, may hold values from -3 to 3
- face_trace: bfloat16 [125, 150], replicated, may hold values from -0.5 to 0.5
- lift: bfloat16 [150, 125], replicated, may hold values from -0.5 to 0.5
- dissip: float32 [5], replicated, may hold values from 0.5 to 2
Outputs:
- indicators: float32 [4096], P(('rx', 'ry'))
Inputs may be any that keep to these rules, and one draw needn't show every extreme that they name: `send_index`: each row lists 16 different local elements of its region. `neighbours`: an entry below 128 is a local element of the element's region; an entry 128 + d * 16 + j appears only at face f = d and only where the region in direction d exists; at a face on the outer boundary the entry is below 128.
All inputs are finite; a program needn't handle non-finite values.
Results may differ from a plain program's by a relative error of at most 0.004.
Values may be sent and summed in bfloat16 or wider, within the bound.
No kernel may reach another device: no remote copies, remote signals or barrier semaphores. Data moves between devices by JAX's collectives and lax.ppermute only.
A program may use at most 128 MiB of HBM per device.

v0:
```python
import functools

import jax
import jax.numpy as jnp
from jax import lax
from jax.experimental import pallas as pl
from jax.experimental.pallas import tpu as pltpu
from jax.sharding import PartitionSpec as P

VARS = 5
MODES = 64
ENR = 125
FACEPTS = 25
FACES = 6
PATCH = 7
LANE = 128
TILES = 5
AXES = ("rx", "ry")
F32 = jnp.float32
BF16 = jnp.bfloat16
VMEM_BYTES = 16 * 1024 * 1024
PRIMAL_AT = ((0, 0), (0, 1), (1, 0), (1, 1), (4, 0))
ADJOINT_AT = ((2, 0), (2, 1), (3, 0), (3, 1), (4, 1))


def swaps(nx, ny):
    def joint(i, j):
        return i * ny + j

    def both(a, b):
        return [(a, b), (b, a)]

    x_even, x_odd, y_even, y_odd = [], [], [], []
    for j in range(ny):
        for i in range(0, nx - 1, 2):
            x_even += both(joint(i, j), joint(i + 1, j))
        for i in range(1, nx - 1, 2):
            x_odd += both(joint(i, j), joint(i + 1, j))
    for i in range(nx):
        for j in range(0, ny - 1, 2):
            y_even += both(joint(i, j), joint(i, j + 1))
        for j in range(1, ny - 1, 2):
            y_odd += both(joint(i, j), joint(i, j + 1))
    for i in {0, nx - 1 if nx % 2 == 0 else 0}:
        for j in range(0, ny - 1, 2):
            x_odd += both(joint(i, j), joint(i, j + 1))
    for j in {0, ny - 1 if ny % 2 == 0 else 0}:
        for i in range(0, nx - 1, 2):
            y_odd += both(joint(i, j), joint(i + 1, j))
    return x_even, x_odd, y_even, y_odd


def parities():
    odd_x = lax.rem(lax.axis_index("rx"), 2)
    odd_y = lax.rem(lax.axis_index("ry"), 2)
    return 1 - odd_x, odd_x, 3 - odd_y, 2 + odd_y


def listed(send_ref, faces):
    sent = send_ref.shape[1]
    rows = [
        jnp.broadcast_to(send_ref[pl.ds(face, 1), :], (sent, sent)) for face in faces
    ]
    table = jnp.concatenate(rows, axis=0)
    lane = lax.broadcasted_iota(jnp.int32, table.shape, 1)
    row = lax.rem(lax.broadcasted_iota(jnp.int32, table.shape, 0), sent)
    column = jnp.sum(jnp.where(lane == row, table, 0).astype(F32), axis=1, keepdims=True)
    return column.astype(jnp.int32)


def onehot(column, width, base):
    lane = lax.broadcasted_iota(jnp.int32, (column.shape[0], width), 1) + base
    return jnp.where(lane == column, 1.0, 0.0).astype(BF16)


def pick(nbr, face):
    lane = lax.broadcasted_iota(jnp.int32, nbr.shape, 1)
    return jnp.sum(jnp.where(lane == face, nbr, 0).astype(F32), axis=1, keepdims=True).astype(jnp.int32)


def dot(a, b):
    return jnp.dot(a, b, preferred_element_type=F32)


def dot_t(a, b):
    return lax.dot_general(a, b, (((1,), (1,)), ((), ())), preferred_element_type=F32)


def pack_kernel(primal_ref, adjoint_ref, send_ref, both_ref, *out_refs):
    sent = send_ref.shape[1]
    primal = primal_ref[...]
    adjoint = adjoint_ref[...]
    both = jnp.concatenate(
        [primal[:, 0:256], adjoint[:, 0:256], primal[:, 256:320], adjoint[:, 256:320]], axis=1
    )
    both_ref[...] = both
    pickings = onehot(listed(send_ref, parities()), primal.shape[0], 0)
    rows = dot(pickings, both).astype(BF16)
    for j, out_ref in enumerate(out_refs):
        out_ref[...] = rows[j * sent : (j + 1) * sent]


def local_kernel(both_ref, nbr_ref, recon_ref, acc_ref, weights_ref, left_ref):
    count = both_ref.shape[0]
    weights_ref[...] = jnp.zeros_like(weights_ref)
    for k in range(PATCH):
        weights_ref[k, 0:MODES, 0:ENR] = recon_ref[k]
        weights_ref[k, MODES : 2 * MODES, LANE : LANE + ENR] = recon_ref[k]
    both = both_ref[...]
    for k in range(PATCH):
        if k == 0:
            rows = both
        else:
            rows = dot(onehot(nbr_ref[:, k - 1 : k], count, 0), both).astype(BF16)
        for t in range(TILES):
            left_ref[t * count : (t + 1) * count, k * LANE : (k + 1) * LANE] = rows[:, t * LANE : (t + 1) * LANE]
    acc_ref[...] = dot(left_ref[...], weights_ref[...].reshape(PATCH * LANE, 2 * LANE))


def enrich_kernel(acc_ref, weights_ref, nbr_ref, send_ref, a_ref, b_ref, c_ref, d_ref, u_ref, z_ref, *out_refs):
    count, sent = nbr_ref.shape[0], send_ref.shape[1]
    faces = parities()
    nbr = nbr_ref[...]
    acc = acc_ref[...]
    for face, ref in zip(faces, (a_ref, b_ref, c_ref, d_ref)):
        hot = onehot(pick(nbr, face), sent, count + face * sent)
        rows = dot(hot, ref[...]).astype(BF16)
        left = jnp.concatenate([rows[:, t * LANE : (t + 1) * LANE] for t in range(TILES)], axis=0)
        acc = acc + dot(left, weights_ref[face + 1])
    for v in range(VARS):
        t, h = PRIMAL_AT[v]
        u_ref[:, v * LANE : (v + 1) * LANE] = acc[t * count : (t + 1) * count, h * LANE : (h + 1) * LANE].astype(BF16)
        t, h = ADJOINT_AT[v]
        z_ref[v * count : (v + 1) * count, :] = acc[t * count : (t + 1) * count, h * LANE : (h + 1) * LANE]
    pickings = onehot(listed(send_ref, faces), count, 0)
    rows = dot(pickings, u_ref[...]).astype(BF16)
    for j, out_ref in enumerate(out_refs):
        out_ref[...] = rows[j * sent : (j + 1) * sent]


def split(x):
    high = x.astype(BF16)
    return high, (x - high.astype(F32)).astype(BF16)


def middle_kernel(
    u_ref, z_ref, nbr_ref, deriv_ref, jacob_ref, trace_ref, lift_ref, dissip_ref, part_ref, c_ref, wide_ref, lift_pad, trace_pad
):
    count = nbr_ref.shape[0]
    points = FACES * FACEPTS
    wide_ref[...] = jnp.zeros_like(wide_ref)
    lift_pad[...] = jnp.zeros_like(lift_pad)
    trace_pad[...] = jnp.zeros_like(trace_pad)
    for a in range(3):
        wide_ref[0:ENR, a * LANE : a * LANE + ENR] = deriv_ref[a]
    wide_ref[0:ENR, 3 * LANE : 3 * LANE + points] = trace_ref[...]
    lift_pad[0:points, 0:ENR] = lift_ref[...]
    trace_pad[0:ENR, 0:points] = trace_ref[...].astype(F32)
    u = u_ref[...]
    stack = jnp.concatenate([u[:, v * LANE : (v + 1) * LANE] for v in range(VARS)], axis=0)
    grads = dot(stack, wide_ref[...])
    z = z_ref[...]
    z_high, z_low = split(z)
    lifted = dot_t(z_high, lift_pad[...]) + dot_t(z_low, lift_pad[...])

    def of(x, v):
        return x[v * count : (v + 1) * count]

    part = jnp.zeros((count, LANE), F32)
    for a in range(3):
        for w in range(VARS):
            zj = jacob_ref[a, 0, w] * of(z, 0)
            for v in range(1, VARS):
                zj = zj + jacob_ref[a, v, w] * of(z, v)
            part = part + zj * of(grads, w)[:, a * LANE : (a + 1) * LANE]
    lane = lax.broadcasted_iota(jnp.int32, (1, 2 * LANE), 1)
    face = lane // FACEPTS
    half = jnp.where(lax.rem(face, 2) == 0, -0.5, 0.5)
    outer_weights = []
    for w in range(VARS):
        mixed = None
        for v in range(VARS):
            coef = half * jnp.where(face < 2, jacob_ref[0, v, w], jnp.where(face < 4, jacob_ref[1, v, w], jacob_ref[2, v, w]))
            term = coef * of(lifted, v)
            mixed = term if mixed is None else mixed + term
        damped = (0.5 * dissip_ref[w]) * of(lifted, w)
        inner = of(grads, w)[:, 3 * LANE :] * (mixed + damped)
        part = part - inner[:, 0:LANE] - inner[:, LANE:]
        outer_weights.append(mixed - damped)
    b_high, b_low = split(jnp.concatenate(outer_weights, axis=0))
    plain = trace_pad[...]
    swapped = jnp.where(
        lax.rem(face, 2) == 0, pltpu.roll(plain, 2 * LANE - FACEPTS, 1), pltpu.roll(plain, FACEPTS, 1)
    )
    blocks = jnp.concatenate([jnp.where(face == f, swapped, 0.0).astype(BF16) for f in range(FACES)], axis=0)
    coef = dot_t(b_high, blocks) + dot_t(b_low, blocks)
    for f in range(FACES):
        mine = coef[:, f * LANE : (f + 1) * LANE]
        rows = dot(onehot(nbr_ref[:, f : f + 1], count, 0), u)
        for v in range(VARS):
            part = part - rows[:, v * LANE : (v + 1) * LANE] * of(mine, v)
        if f < 4:
            c_ref[f] = mine
    part_ref[...] = part


def last_kernel(part_ref, coef_ref, nbr_ref, a_ref, b_ref, c_ref, d_ref, out_ref):
    count, sent = nbr_ref.shape[0], a_ref.shape[0]
    nbr = nbr_ref[...]
    part = part_ref[...]
    for face, ref in zip(parities(), (a_ref, b_ref, c_ref, d_ref)):
        hot = onehot(pick(nbr, face), sent, count + face * sent)
        rows = dot(hot, ref[...])
        coef = coef_ref[face]
        for v in range(VARS):
            part = part - rows[:, v * LANE : (v + 1) * LANE] * coef[v * count : (v + 1) * count]
    out_ref[...] = 0.04 * jnp.sum(part.T, axis=0, keepdims=True)


def call(kernel, outs, specs=None, scratch=(), flops=0, moved=0):
    def run(*args):
        places = specs or [pltpu.VMEM] * len(args)
        return pl.pallas_call(
            kernel,
            out_shape=outs,
            in_specs=[pl.BlockSpec(memory_space=m) for m in places],
            out_specs=jax.tree.map(lambda _: pl.BlockSpec(memory_space=pltpu.VMEM), outs),
            scratch_shapes=scratch,
            compiler_params=pltpu.CompilerParams(vmem_limit_bytes=VMEM_BYTES),
            cost_estimate=pl.CostEstimate(flops=flops, bytes_accessed=moved, transcendentals=0),
        )(*args)

    return run


def shards(mesh, primal, adjoint, send_index, neighbours, recon, deriv, jacob, face_trace, lift, dissip):
    count, sent = primal.shape[0], send_index.shape[1]
    perms = swaps(mesh.shape["rx"], mesh.shape["ry"])
    wide = TILES * LANE
    shape = jax.ShapeDtypeStruct
    message = shape((sent, wide), BF16)
    both, *first = call(pack_kernel, [shape((count, wide), BF16)] + [message] * 4)(primal, adjoint, send_index)
    got = [lax.ppermute(m, AXES, pairs) for m, pairs in zip(first, perms)]
    acc, weights = call(
        local_kernel,
        [shape((TILES * count, 2 * LANE), F32), shape((PATCH, LANE, 2 * LANE), BF16)],
        scratch=[pltpu.VMEM((TILES * count, PATCH * LANE), BF16)],
        flops=10**9,
        moved=10**6,
    )(both, neighbours, recon)
    u4, z4, *second = call(
        enrich_kernel, [shape((count, wide), BF16), shape((VARS * count, LANE), F32)] + [message] * 4
    )(acc, weights, neighbours, send_index, *got)
    got = [lax.ppermute(m, AXES, pairs) for m, pairs in zip(second, perms)]
    smem, vmem = pltpu.SMEM, pltpu.VMEM
    part, coef = call(
        middle_kernel,
        [shape((count, LANE), F32), shape((4, VARS * count, LANE), F32)],
        specs=[vmem, vmem, vmem, vmem, smem, vmem, vmem, smem],
        scratch=[
            pltpu.VMEM((LANE, 5 * LANE), BF16),
            pltpu.VMEM((2 * LANE, LANE), BF16),
            pltpu.VMEM((LANE, 2 * LANE), F32),
        ],
        flops=10**9,
        moved=10**6,
    )(u4, z4, neighbours, deriv, jacob, face_trace, lift, dissip)
    out = call(last_kernel, shape((1, count), F32))(part, coef, neighbours, *got)
    return out.reshape(count)


def solution(mesh):
    rows = P(AXES, None)
    return jax.shard_map(
        functools.partial(shards, mesh),
        mesh=mesh,
        in_specs=(rows, rows, rows, rows, P(), P(), P(), P(), P(), P()),
        out_specs=P(AXES),
        check_vma=False,
    )
```

profile of v0, /device:TPU:0, one launch (start us, length us, event | category | flops | bytes accessed | tf_op | source)
XLA Modules:
  0.0 19.5 jit_solution(14599651265325382713)
XLA Ops:
  0.0 1.0 %copy.11.primal_ref = bf16[128,320]{1,0:T(8,128)(2,1)S(1)} copy(bf16[128,320]{0,1:T(8,128)(2,1)} %param.10) | data formatting | bytes 163840 | tf_op args[0]
  1.0 1.0 %copy.12.adjoint_ref = bf16[128,320]{1,0:T(8,128)(2,1)S(1)} copy(bf16[128,320]{0,1:T(8,128)(2,1)} %param.11) | data formatting | bytes 163840 | tf_op args[1]
  2.0 0.0 copy-start
  2.0 0.7 %copy-done = s32[4,16]{1,0:T(4,128)S(1)} copy-done((s32[4,16]{1,0:T(4,128)S(1)}, s32[4,16]{1,0:T(4,128)}, u32[]{:S(2)}) %copy-start) | copy-done | bytes 280
  2.7 0.2 %shard_map.100 = (bf16[128,640]{1,0:T(8,128)(2,1)S(1)}, bf16[16,640]{1,0:T(8,128)(2,1)S(1)}, bf16[16,640]{1,0:T(8,128)(2,1)S(1)}, bf16[16,640]{1,0:T(8,128)(2,1)S(1)}, bf16[16,640]{1,0:T(8,128)(2,1)S(1)}) custom-call(bf16[128,320]{1,0:T(8,128)(2,1)S(1)} %copy.11.primal_ref, bf16[128,320]{1,0:T(8,128)(2,1)S(1)} %copy.12.adjoint_ref, s32[4,16]{1,0:T(4,128)S(1)} %copy-done), custom_call_target="tpu_custom_call" | custom-call | tf_op jit(solution)/shard_map/pallas_call | solution.py:223
  2.9 0.5 %collective-permute-start = (bf16[16,640]{1,0:T(8,128)(2,1)S(1)}, bf16[16,640]{1,0:T(8,128)(2,1)S(1)}, u32[]{:S(2)}, u32[]{:S(2)}) collective-permute-start(bf16[16,640]{1,0:T(8,128)(2,1)S(1)} %get-tuple-element.23), channel_id=1, source_target_pairs={{0,4},{4,0},{8,12},{12,8},{16,20},{20,16},{24,28},{28,24},{1,5},{5... | collective-permute-start | bytes 61448 | tf_op jit(solution)/shard_map/ppermute | solution.py:243
  3.5 2.6 %collective-permute-start.1 = (bf16[16,640]{1,0:T(8,128)(2,1)S(1)}, bf16[16,640]{1,0:T(8,128)(2,1)S(1)}, u32[]{:S(2)}, u32[]{:S(2)}) collective-permute-start(bf16[16,640]{1,0:T(8,128)(2,1)S(1)} %get-tuple-element.24), channel_id=1, source_target_pairs={{4,8},{8,4},{12,16},{16,12},{20,24},{24,20},{5,9},{9,5},{13,17},{1... | collective-permute-start | bytes 61448 | tf_op jit(solution)/shard_map/ppermute | solution.py:243
  6.0 0.1 collective-permute-start.2
  6.1 1.3 %collective-permute-start.3 = (bf16[16,640]{1,0:T(8,128)(2,1)S(1)}, bf16[16,640]{1,0:T(8,128)(2,1)S(1)}, u32[]{:S(2)}, u32[]{:S(2)}) collective-permute-start(bf16[16,640]{1,0:T(8,128)(2,1)S(1)} %get-tuple-element.26), channel_id=1, source_target_pairs={{1,2},{2,1},{5,6},{6,5},{9,10},{10,9},{13,14},{14,13},{17,18},{18,... | collective-permute-start | bytes 61448 | tf_op jit(solution)/shard_map/ppermute | solution.py:243
  7.4 0.8 %copy.13.nbr_ref = s32[128,6]{1,0:T(8,128)S(1)} copy(s32[128,6]{0,1:T(8,128)} %param.13) | data formatting | bytes 6144 | tf_op args[3]
  8.2 0.9 %copy-done.2 = bf16[7,64,125]{2,1,0:T(8,128)(2,1)S(1)} copy-done((bf16[7,64,125]{2,1,0:T(8,128)(2,1)S(1)}, bf16[7,64,125]{2,1,0:T(8,128)(2,1)}, u32[]{:S(2)}) %copy-start.2) | copy-done | bytes 112024
  9.1 0.8 %shard_map.101 = (f32[640,256]{1,0:T(8,128)S(1)}, bf16[7,128,256]{2,1,0:T(8,128)(2,1)S(1)}) custom-call(bf16[128,640]{1,0:T(8,128)(2,1)S(1)} %get-tuple-element.20.both_ref, s32[128,6]{1,0:T(8,128)S(1)} %copy.13.nbr_ref, bf16[7,64,125]{2,1,0:T(8,128)(2,1)S(1)} %copy-done.2), custom_call_target="tpu_custom_call" | custom-call | flops 1000000000 | bytes 1000000 | tf_op jit(solution)/shard_map/pallas_call | solution.py:223
  10.0 0.0 copy-start.3
  10.0 0.0 copy-start.4
  10.0 0.0 copy-start.5
  10.0 0.1 copy.17.trace_ref
  10.2 0.0 collective-permute-done.1.b_ref
  10.2 1.3 %shard_map.102 = (bf16[128,640]{1,0:T(8,128)(2,1)S(1)}, f32[640,128]{1,0:T(8,128)S(1)}, bf16[16,640]{1,0:T(8,128)(2,1)S(1)}, bf16[16,640]{1,0:T(8,128)(2,1)S(1)}...) custom-call(f32[640,256]{1,0:T(8,128)S(1)} %get-tuple-element.21.acc_ref, ...), custom_call_target="tpu_custom_call" | custom-call | tf_op jit(solution)/shard_map/pallas_call | solution.py:223
  11.5 0.0 collective-permute-start.4
  11.5 2.7 %collective-permute-start.5 = (bf16[16,640]{1,0:T(8,128)(2,1)S(1)}, bf16[16,640]{1,0:T(8,128)(2,1)S(1)}, u32[]{:S(2)}, u32[]{:S(2)}) collective-permute-start(bf16[16,640]{1,0:T(8,128)(2,1)S(1)} %get-tuple-element.32), channel_id=1, source_target_pairs={{4,8},{8,4},{12,16},{16,12},{20,24},{24,20},{5,9},{9,5},{13,17},{1... | collective-permute-start | bytes 61448 | tf_op jit(solution)/shard_map/ppermute | solution.py:254
  14.2 0.0 collective-permute-start.6
  14.2 1.4 %collective-permute-start.7 = (bf16[16,640]{1,0:T(8,128)(2,1)S(1)}, bf16[16,640]{1,0:T(8,128)(2,1)S(1)}, u32[]{:S(2)}, u32[]{:S(2)}) collective-permute-start(bf16[16,640]{1,0:T(8,128)(2,1)S(1)} %get-tuple-element.34), channel_id=1, source_target_pairs={{1,2},{2,1},{5,6},{6,5},{9,10},{10,9},{13,14},{14,13},{17,18},{18,... | collective-permute-start | bytes 61448 | tf_op jit(solution)/shard_map/ppermute | solution.py:254
  15.6 2.8 %shard_map.103 = (f32[128,128]{1,0:T(8,128)S(1)}, f32[4,640,128]{2,1,0:T(8,128)S(1)}) custom-call(bf16[128,640]{1,0:T(8,128)(2,1)S(1)} %get-tuple-element.27.u_ref, f32[640,128]{1,0:T(8,128)S(1)} %get-tuple-element.28.z_ref, s32[128,6]{1,0:T(8,128)S(1)} %copy.13.nbr_ref, bf16[3,125,125]{2,1,0:T(8,128)(2,1)S(1)} %copy-done.3, f32[3,5,5]{2,1,0:T(8,128)S(1)} %copy.16.jacob_ref, ...), custom_call_target="tpu_custom_call" | custom-call | flops 1000000000 | bytes 1000000 | tf_op jit(solution)/shard_map/pallas_call | solution.py:223
  18.5 1.0 %shard_map.104 = f32[1,128]{1,0:T(1,128)} custom-call(f32[128,128]{1,0:T(8,128)S(1)} %get-tuple-element.29.part_ref, f32[4,640,128]{2,1,0:T(8,128)S(1)} %get-tuple-element.30.coef_ref, s32[128,6]{1,0:T(8,128)S(1)} %copy.13.nbr_ref, bf16[16,640]{1,0:T(8,128)(2,1)S(1)} %collective-permute-done.4.a_ref, bf16[16,640]{1,0:T(8,128)(2,1)S(1)} %collective-permute-done.5.b_ref, ...), custom_call_target="tpu_custom_call" | custom-call | tf_op jit(solution)/shard_map/pallas_call | solution.py:223
  (18 shorter events, 0.0 us)
Async XLA Ops:
  2.0 0.7 %copy-start = (s32[4,16]{1,0:T(4,128)S(1)}, s32[4,16]{1,0:T(4,128)}, u32[]{:S(2)}) copy-start(s32[4,16]{1,0:T(4,128)} %send_ref.3) | copy-start | bytes 772
  2.9 7.2 %collective-permute-start = (bf16[16,640]{1,0:T(8,128)(2,1)S(1)}, bf16[16,640]{1,0:T(8,128)(2,1)S(1)}, u32[]{:S(2)}, u32[]{:S(2)}) collective-permute-start(bf16[16,640]{1,0:T(8,128)(2,1)S(1)} %get-tuple-element.23), channel_id=1, source_target_pairs={{0,4},{4,0},{8,12},{12,8},{16,20},{20,16},{24,28},{28,24},{1,5},{5... | collective-permute-start | bytes 61448 | tf_op jit(solution)/shard_map/ppermute | solution.py:243
  3.5 6.7 %collective-permute-start.1 = (bf16[16,640]{1,0:T(8,128)(2,1)S(1)}, bf16[16,640]{1,0:T(8,128)(2,1)S(1)}, u32[]{:S(2)}, u32[]{:S(2)}) collective-permute-start(bf16[16,640]{1,0:T(8,128)(2,1)S(1)} %get-tuple-element.24), channel_id=1, source_target_pairs={{4,8},{8,4},{12,16},{16,12},{20,24},{24,20},{5,9},{9,5},{13,17},{1... | collective-permute-start | bytes 61448 | tf_op jit(solution)/shard_map/ppermute | solution.py:243
  6.0 4.2 %collective-permute-start.2 = (bf16[16,640]{1,0:T(8,128)(2,1)S(1)}, bf16[16,640]{1,0:T(8,128)(2,1)S(1)}, u32[]{:S(2)}, u32[]{:S(2)}) collective-permute-start(bf16[16,640]{1,0:T(8,128)(2,1)S(1)} %get-tuple-element.25), channel_id=1, source_target_pairs={{0,1},{1,0},{2,3},{3,2},{4,5},{5,4},{6,7},{7,6},{8,9},{9,8},{10,11... | collective-permute-start | bytes 61448 | tf_op jit(solution)/shard_map/ppermute | solution.py:243
  6.1 4.1 %collective-permute-start.3 = (bf16[16,640]{1,0:T(8,128)(2,1)S(1)}, bf16[16,640]{1,0:T(8,128)(2,1)S(1)}, u32[]{:S(2)}, u32[]{:S(2)}) collective-permute-start(bf16[16,640]{1,0:T(8,128)(2,1)S(1)} %get-tuple-element.26), channel_id=1, source_target_pairs={{1,2},{2,1},{5,6},{6,5},{9,10},{10,9},{13,14},{14,13},{17,18},{18,... | collective-permute-start | bytes 61448 | tf_op jit(solution)/shard_map/ppermute | solution.py:243
  8.2 0.9 %copy-start.2 = (bf16[7,64,125]{2,1,0:T(8,128)(2,1)S(1)}, bf16[7,64,125]{2,1,0:T(8,128)(2,1)}, u32[]{:S(2)}) copy-start(bf16[7,64,125]{2,1,0:T(8,128)(2,1)} %recon_ref.1) | copy-start | bytes 336004
  9.1 0.8 %copy-start.7 = (f32[3,5,5]{2,0,1:T(4,128)S(1)}, f32[3,5,5]{2,0,1:T(4,128)}, u32[]{:S(2)}) copy-start(f32[3,5,5]{2,0,1:T(4,128)} %param.16) | copy-start | bytes 904
  9.1 0.9 %copy-start.6 = (bf16[125,150]{0,1:T(8,128)(2,1)S(1)}, bf16[125,150]{0,1:T(8,128)(2,1)}, u32[]{:S(2)}) copy-start(bf16[125,150]{0,1:T(8,128)(2,1)} %param.17) | copy-start | bytes 112504
  9.1 1.1 %copy-start.1 = (s32[4,16]{1,0:T(4,128)S(1)}, s32[4,16]{1,0:T(4,128)}, u32[]{:S(2)}) copy-start(s32[4,16]{1,0:T(4,128)} %send_ref.3) | copy-start | bytes 772
  10.0 5.6 %copy-start.3 = (bf16[3,125,125]{2,1,0:T(8,128)(2,1)S(1)}, bf16[3,125,125]{2,1,0:T(8,128)(2,1)}, u32[]{:S(2)}) copy-start(bf16[3,125,125]{2,1,0:T(8,128)(2,1)} %deriv_ref.1) | copy-start | bytes 281254
  10.0 5.6 %copy-start.4 = (bf16[150,125]{1,0:T(8,128)(2,1)S(1)}, bf16[150,125]{1,0:T(8,128)(2,1)}, u32[]{:S(2)}) copy-start(bf16[150,125]{1,0:T(8,128)(2,1)} %lift_ref.1) | copy-start | bytes 112504
  10.0 5.6 %copy-start.5 = (f32[5]{0:T(128)S(1)}, f32[5]{0:T(128)}, u32[]{:S(2)}) copy-start(f32[5]{0:T(128)} %dissip_ref.1) | copy-start | bytes 64
  11.5 6.9 %collective-permute-start.4 = (bf16[16,640]{1,0:T(8,128)(2,1)S(1)}, bf16[16,640]{1,0:T(8,128)(2,1)S(1)}, u32[]{:S(2)}, u32[]{:S(2)}) collective-permute-start(bf16[16,640]{1,0:T(8,128)(2,1)S(1)} %get-tuple-element.31), channel_id=1, source_target_pairs={{0,4},{4,0},{8,12},{12,8},{16,20},{20,16},{24,28},{28,24},{1,5},{5... | collective-permute-start | bytes 61448 | tf_op jit(solution)/shard_map/ppermute | solution.py:254
  11.5 6.9 %collective-permute-start.5 = (bf16[16,640]{1,0:T(8,128)(2,1)S(1)}, bf16[16,640]{1,0:T(8,128)(2,1)S(1)}, u32[]{:S(2)}, u32[]{:S(2)}) collective-permute-start(bf16[16,640]{1,0:T(8,128)(2,1)S(1)} %get-tuple-element.32), channel_id=1, source_target_pairs={{4,8},{8,4},{12,16},{16,12},{20,24},{24,20},{5,9},{9,5},{13,17},{1... | collective-permute-start | bytes 61448 | tf_op jit(solution)/shard_map/ppermute | solution.py:254
  14.2 4.2 %collective-permute-start.6 = (bf16[16,640]{1,0:T(8,128)(2,1)S(1)}, bf16[16,640]{1,0:T(8,128)(2,1)S(1)}, u32[]{:S(2)}, u32[]{:S(2)}) collective-permute-start(bf16[16,640]{1,0:T(8,128)(2,1)S(1)} %get-tuple-element.33), channel_id=1, source_target_pairs={{0,1},{1,0},{2,3},{3,2},{4,5},{5,4},{6,7},{7,6},{8,9},{9,8},{10,11... | collective-permute-start | bytes 61448 | tf_op jit(solution)/shard_map/ppermute | solution.py:254
  14.2 4.2 %collective-permute-start.7 = (bf16[16,640]{1,0:T(8,128)(2,1)S(1)}, bf16[16,640]{1,0:T(8,128)(2,1)S(1)}, u32[]{:S(2)}, u32[]{:S(2)}) collective-permute-start(bf16[16,640]{1,0:T(8,128)(2,1)S(1)} %get-tuple-element.34), channel_id=1, source_target_pairs={{1,2},{2,1},{5,6},{6,5},{9,10},{10,9},{13,14},{14,13},{17,18},{18,... | collective-permute-start | bytes 61448 | tf_op jit(solution)/shard_map/ppermute | solution.py:254
where the time goes:
time: 19.7 us; the launch traced here: 19.5 us
  starting transfers between devices  8.59 us (44%)
  Pallas kernels  6.18 us (31%)
  local copies, waits for them, and re-layouts  4.52 us (23%)
    pallas_call x5, Pallas kernels, run(): pl.pallas_call(kernel, out_shape=outs, in_specs=[pl.BlockSpec(memory_spac...  6.18 us
    unnamed x21, local copies, waits for them, and re-layouts  4.52 us
    ppermute x4, starting transfers between devices, shards(): got = [lax.ppermute(m, AXES, pairs) for m, pairs in zip(first, perms)]  4.48 us
    ppermute x4, starting transfers between devices, shards(): got = [lax.ppermute(m, AXES, pairs) for m, pairs in zip(second, perms)]  4.1 us
  transfers between devices with their start and end apart: 8, of which 0 were waited for; matrix products, arithmetic and copies ran while one was open for 5% of the time, Pallas kernels for 19%

commit v1 on v0

v1 whole, which is shorter than its diff:
```python
import functools

import jax
import jax.numpy as jnp
from jax import lax
from jax.experimental import pallas as pl
from jax.experimental.pallas import tpu as pltpu
from jax.sharding import PartitionSpec as P

VARS = 5
MODES = 64
ENR = 125
FACEPTS = 25
FACES = 6
PATCH = 7
LANE = 128
WIDE = VARS * LANE
FIELD = VARS * MODES
POINTS = FACES * FACEPTS
AXES = ("rx", "ry")
F32 = jnp.float32
BF16 = jnp.bfloat16
VMEM_BYTES = 16 * 1024 * 1024


def swaps(nx, ny):
    def joint(i, j):
        return i * ny + j

    def both(a, b):
        return [(a, b), (b, a)]

    x_even, x_odd, y_even, y_odd = [], [], [], []
    for j in range(ny):
        for i in range(0, nx - 1, 2):
            x_even += both(joint(i, j), joint(i + 1, j))
        for i in range(1, nx - 1, 2):
            x_odd += both(joint(i, j), joint(i + 1, j))
    for i in range(nx):
        for j in range(0, ny - 1, 2):
            y_even += both(joint(i, j), joint(i, j + 1))
        for j in range(1, ny - 1, 2):
            y_odd += both(joint(i, j), joint(i, j + 1))
    for i in {0, nx - 1 if nx % 2 == 0 else 0}:
        for j in range(0, ny - 1, 2):
            x_odd += both(joint(i, j), joint(i, j + 1))
    for j in {0, ny - 1 if ny % 2 == 0 else 0}:
        for i in range(0, nx - 1, 2):
            y_odd += both(joint(i, j), joint(i + 1, j))
    return x_even, x_odd, y_even, y_odd


def directions():
    odd_x = lax.rem(lax.axis_index("rx"), 2)
    odd_y = lax.rem(lax.axis_index("ry"), 2)
    return 1 - odd_x, odd_x, 3 - odd_y, 2 + odd_y


def iota(shape, dim):
    return lax.broadcasted_iota(jnp.int32, shape, dim)


def hot(rows, wanted):
    return jnp.where(rows == wanted, 1.0, 0.0)


def dot(a, b):
    return jnp.dot(a, b, preferred_element_type=F32)


def dot_rows(a, b):
    return lax.dot_general(a, b, (((0,), (0,)), ((), ())), preferred_element_type=F32)


def dot_lanes(a, b):
    return lax.dot_general(a, b, (((1,), (1,)), ((), ())), preferred_element_type=F32)


def lanes(x, i, width=LANE):
    return x[:, i * width : (i + 1) * width]


def rows(x, i, height=LANE):
    return x[i * height : (i + 1) * height]


def mask_kernel(mask_ref):
    shape = mask_ref.shape
    mask_ref[...] = hot(lax.rem(iota(shape, 0), shape[1]), iota(shape, 1))


def pack_kernel(mask_ref, primal_ref, adjoint_ref, send_ref, pick_ref, *messages):
    count, sent = primal_ref.shape[1], send_ref.shape[1]
    table = jnp.concatenate(
        [jnp.broadcast_to(send_ref[pl.ds(face, 1), :], (sent, sent)) for face in directions()], axis=0
    )
    column = jnp.sum(table.astype(F32) * mask_ref[...], axis=1, keepdims=True).astype(jnp.int32)
    pick = hot(iota((4 * sent, count), 1), column).astype(BF16)
    pick_ref[...] = pick
    state = jnp.concatenate([primal_ref[...], adjoint_ref[...]], axis=0)
    packed = dot_lanes(pick, state).astype(BF16)
    for j, out_ref in enumerate(messages):
        out_ref[...] = rows(packed, j, sent)


def local_kernel(
    primal_ref,
    adjoint_ref,
    nbr_ref,
    recon_ref,
    deriv_ref,
    lift_ref,
    trace_ref,
    pick_ref,
    near_ref,
    listed_ref,
    hot_ref,
    listed_hot_ref,
    far_recon_ref,
    pair_recon_ref,
    weights_ref,
    back_ref,
    gathered_ref,
    tall_ref,
    square_ref,
    wide_ref,
    trace_pad_ref,
):
    count = nbr_ref.shape[1]
    sent = pick_ref.shape[0] // 4
    faces = directions()
    tall_ref[...] = jnp.zeros_like(tall_ref)
    for k in range(PATCH):
        tall_ref[k * MODES : (k + 1) * MODES, 0:ENR] = recon_ref[k].astype(F32)
    recon_t = tall_ref[...].T.astype(BF16)[:, 0 : PATCH * MODES]
    pair_recon_ref[...] = jnp.zeros_like(pair_recon_ref)
    for j, face in enumerate(faces):
        mine = tall_ref[pl.ds((face + 1) * MODES, MODES), :]
        far_recon_ref[:, j * MODES : (j + 1) * MODES] = mine.T.astype(BF16)
        pair_recon_ref[j * LANE : j * LANE + MODES, 0:LANE] = mine.astype(BF16)
        pair_recon_ref[j * LANE + MODES : (j + 1) * LANE, LANE:] = mine.astype(BF16)
    hots = [
        hot(iota((sent, count), 0) + (count + face * sent), nbr_ref[pl.ds(face, 1), :]).astype(BF16)
        for face in faces
    ]
    hot_ref[...] = jnp.zeros_like(hot_ref)
    for j in range(4):
        hot_ref[j * sent : (j + 1) * sent, j * count : (j + 1) * count] = hots[j]
    pick = pick_ref[...]
    listed = dot_lanes(pick, jnp.concatenate(hots, axis=0))
    source = iota((1, 4 * sent), 1) // sent
    for j in range(4):
        listed_hot_ref[j * 4 * sent : (j + 1) * 4 * sent, :] = jnp.where(source == j, listed, 0.0).astype(BF16)
    local = jnp.concatenate(
        [hot(iota((count, count), 0), nbr_ref[f : f + 1, :]).astype(BF16) for f in range(FACES)], axis=1
    )
    for i, ref in enumerate((primal_ref, adjoint_ref)):
        state = ref[...]
        found = dot(state, local).astype(BF16)
        for v in range(VARS):
            place = slice((i * VARS + v) * count, (i * VARS + v + 1) * count)
            gathered_ref[0:MODES, place] = rows(state, v, MODES)
            for f in range(FACES):
                gathered_ref[(f + 1) * MODES : (f + 2) * MODES, place] = rows(lanes(found, f), v, MODES)
    near = dot(recon_t, gathered_ref[...])
    near_ref[...] = near
    stack = jnp.concatenate([lanes(near, v) for v in range(VARS)], axis=0)
    high = stack.astype(BF16)
    low = (stack - high.astype(F32)).astype(BF16)
    listed_ref[...] = dot_lanes(pick, high) + dot_lanes(pick, low)
    wide_ref[...] = jnp.zeros_like(wide_ref)
    wide_ref[0:POINTS, 0:ENR] = lift_ref[...].astype(F32)
    trace_pad_ref[...] = jnp.zeros_like(trace_pad_ref)
    trace_pad_ref[0:POINTS, 0:ENR] = trace_ref[...]
    lift_t = wide_ref[...].T
    face = iota((1, 2 * LANE), 1) // FACEPTS
    up = pltpu.roll(lift_t, FACEPTS, 1)
    down = pltpu.roll(lift_t, 2 * LANE - FACEPTS, 1)
    blocks = []
    for a in range(3):
        half = jnp.where(face == 2 * a, 0.5, jnp.where(face == 2 * a + 1, -0.5, 0.0))
        blocks.append(lift_t * half)
    blocks.append(-0.5 * lift_t)
    for f in range(FACES):
        blocks.append(jnp.where(face == f ^ 1, down if f % 2 else up, 0.0) * 0.5)
    products = dot(jnp.concatenate(blocks, axis=0).astype(BF16), trace_pad_ref[...])
    weights_ref[...] = jnp.zeros_like(weights_ref)
    square_ref[...] = jnp.zeros_like(square_ref)
    for a in range(3):
        square_ref[0:ENR, 0:ENR] = deriv_ref[a].astype(F32)
        weights_ref[a * LANE : (a + 1) * LANE, 0:LANE] = (
            square_ref[...].T + products[a * LANE : (a + 1) * LANE]
        ).astype(BF16)
    weights_ref[3 * LANE : 4 * LANE, 0:LANE] = products[3 * LANE : 4 * LANE].astype(BF16)
    for f in range(FACES):
        across = products[(4 + f) * LANE : (5 + f) * LANE]
        place = slice((f + 1) * LANE, (f + 2) * LANE)
        row = (f // 2) * LANE
        weights_ref[row : row + LANE, place] = (-across if f % 2 else across).astype(BF16)
        weights_ref[3 * LANE : 4 * LANE, place] = across.astype(BF16)
        if f < 4:
            back_ref[f] = across.T.astype(BF16)


def listed_kernel(near_ref, hot_ref, recon_ref, a_ref, b_ref, c_ref, d_ref, *messages):
    sent = a_ref.shape[0]
    packed = jnp.concatenate([ref[:, 0 : 3 * LANE] for ref in (a_ref, b_ref, c_ref, d_ref)], axis=0)
    found = dot(hot_ref[...], packed).astype(BF16)
    left = jnp.concatenate(
        [jnp.concatenate([lanes(rows(found, j, 4 * sent), t) for j in range(4)], axis=1) for t in range(3)], axis=0
    )
    far = dot(left, recon_ref[...])
    for v in range(VARS):
        state = lanes(rows(far, v // 2, 4 * sent), v % 2) + lanes(near_ref[...], v)
        for j, out_ref in enumerate(messages):
            out_ref[:, v * LANE : (v + 1) * LANE] = rows(state, j, sent).astype(BF16)


def middle_kernel(
    near_ref,
    hot_ref,
    recon_ref,
    nbr_ref,
    weights_ref,
    back_ref,
    jacob_ref,
    dissip_ref,
    a_ref,
    b_ref,
    c_ref,
    d_ref,
    part_ref,
    coef_ref,
    right_ref,
    state_ref,
    signed_ref,
):
    count = nbr_ref.shape[1]
    packed = jnp.concatenate([ref[...] for ref in (a_ref, b_ref, c_ref, d_ref)], axis=0)
    found = dot_rows(packed, hot_ref[...]).astype(BF16)
    far = [
        jnp.concatenate(
            [
                jnp.concatenate([rows(lanes(found, j), i * VARS + v, MODES) for v in range(VARS)], axis=1)
                for j in range(4)
            ],
            axis=0,
        )
        for i in range(2)
    ]
    u = (near_ref[:, 0:WIDE] + dot(recon_ref[...], far[0])).astype(BF16)
    state_ref[...] = near_ref[:, WIDE:] + dot(recon_ref[...], far[1])
    right_ref[0:LANE, :] = u
    stack = jnp.concatenate([lanes(u, v) for v in range(VARS)], axis=0)
    local = jnp.concatenate(
        [hot(iota((count, count), 0), nbr_ref[f : f + 1, :]).astype(BF16) for f in range(FACES)], axis=1
    )
    across = dot(stack, local).astype(BF16)
    for f in range(FACES):
        for v in range(VARS):
            right_ref[(f + 1) * LANE : (f + 2) * LANE, v * count : (v + 1) * count] = rows(lanes(across, f), v)
    mixed = dot(weights_ref[...], right_ref[...])
    part = jnp.zeros((LANE, count), F32)
    for w in range(VARS):
        place = slice(w * count, (w + 1) * count)
        damped = dissip_ref[w] * state_ref[:, place]
        part = part + damped * mixed[3 * LANE :, place]
        for a in range(3):
            turned = jacob_ref[0, a, w] * state_ref[:, 0:count]
            for v in range(1, VARS):
                turned = turned + jacob_ref[v, a, w] * state_ref[:, v * count : (v + 1) * count]
            part = part + turned * mixed[a * LANE : (a + 1) * LANE, place]
            if a < 2:
                signed_ref[2 * a, :, place] = (damped + turned).astype(BF16)
                signed_ref[2 * a + 1, :, place] = (damped - turned).astype(BF16)
    for f in range(4):
        coef = dot(back_ref[f], signed_ref[f])
        for v in range(VARS):
            coef_ref[f, v * LANE : (v + 1) * LANE, :] = lanes(coef, v)
    part_ref[...] = jnp.sum(part.reshape(LANE // 8, 8, count), axis=0)


def last_kernel(part_ref, coef_ref, hot_ref, a_ref, b_ref, c_ref, d_ref, out_ref):
    packed = jnp.concatenate([ref[...] for ref in (a_ref, b_ref, c_ref, d_ref)], axis=0)
    found = dot_rows(packed, hot_ref[...])
    terms = lanes(found, 0) * coef_ref[directions()[0]]
    for j, face in enumerate(directions()):
        if j:
            terms = terms + lanes(found, j) * coef_ref[face]
    total = part_ref[...] + jnp.sum(terms.reshape(WIDE // 8, 8, terms.shape[1]), axis=0)
    out_ref[...] = 0.04 * jnp.sum(total, axis=0, keepdims=True)


def call(kernel, outs, specs=None, scratch=(), flops=10**6, moved=10**5, grant=VMEM_BYTES):
    def run(*args):
        places = specs or [pltpu.VMEM] * len(args)
        return pl.pallas_call(
            kernel,
            out_shape=outs,
            in_specs=[pl.BlockSpec(memory_space=m) for m in places],
            out_specs=jax.tree.map(lambda _: pl.BlockSpec(memory_space=pltpu.VMEM), outs),
            scratch_shapes=scratch,
            compiler_params=pltpu.CompilerParams(vmem_limit_bytes=grant),
            cost_estimate=pl.CostEstimate(flops=flops, bytes_accessed=moved, transcendentals=0),
        )(*args)

    return run


def shards(mesh, primal, adjoint, send_index, neighbours, recon, deriv, jacob, face_trace, lift, dissip):
    count, sent = primal.shape[0], send_index.shape[1]
    perms = swaps(mesh.shape["rx"], mesh.shape["ry"])
    shape, vmem, smem = jax.ShapeDtypeStruct, pltpu.VMEM, pltpu.SMEM
    message = shape((sent, WIDE), BF16)
    primal_t, adjoint_t, nbr = primal.T, adjoint.T, neighbours.T
    mask = call(mask_kernel, shape((4 * sent, sent), F32), flops=5 * 10**9)()
    pick, *first = call(pack_kernel, [shape((4 * sent, count), BF16)] + [message] * 4, flops=10**9)(
        mask, primal_t, adjoint_t, send_index
    )
    got = [lax.ppermute(m, AXES, pairs) for m, pairs in zip(first, perms)]
    near, listed, hots, listed_hots, far_recon, pair_recon, weights, back = call(
        local_kernel,
        [
            shape((LANE, 2 * WIDE), F32),
            shape((4 * sent, WIDE), F32),
            shape((4 * sent, 4 * count), BF16),
            shape((16 * sent, 4 * sent), BF16),
            shape((LANE, 4 * MODES), BF16),
            shape((4 * LANE, 2 * LANE), BF16),
            shape((4 * LANE, 7 * LANE), BF16),
            shape((4, LANE, LANE), BF16),
        ],
        scratch=[
            vmem((PATCH * MODES, 2 * WIDE), BF16),
            vmem((4 * LANE, LANE), F32),
            vmem((LANE, LANE), F32),
            vmem((2 * LANE, LANE), F32),
            vmem((2 * LANE, LANE), BF16),
        ],
        flops=10**9,
        moved=10**6,
    )(primal_t, adjoint_t, nbr, recon, deriv, lift, face_trace.T, pick)
    second = call(listed_kernel, [message] * 4)(listed, listed_hots, pair_recon, *got)
    got_more = [lax.ppermute(m, AXES, pairs) for m, pairs in zip(second, perms)]
    part, coef = call(
        middle_kernel,
        [shape((8, count), F32), shape((4, WIDE, count), F32)],
        specs=[vmem] * 6 + [smem] * 2 + [vmem] * 4,
        scratch=[vmem((7 * LANE, WIDE), BF16), vmem((LANE, WIDE), F32), vmem((4, LANE, WIDE), BF16)],
        flops=10**9,
        moved=10**6,
    )(near, hots, far_recon, nbr, weights, back, jacob.transpose(1, 0, 2), dissip, *got)
    out = call(last_kernel, shape((1, count), F32))(part, coef, hots, *got_more)
    return out.reshape(count)


def solution(mesh):
    rows = P(AXES, None)
    return jax.shard_map(
        functools.partial(shards, mesh),
        mesh=mesh,
        in_specs=(rows, rows, rows, rows, P(), P(), P(), P(), P(), P()),
        out_specs=P(AXES),
        check_vma=False,
    )
```

time: 19.7 us -> 16.4 us (0.83)
  local copies, waits for them, and re-layouts: 4.52 us -> 0.95 us
  waiting for transfers between devices: 0.02 us -> 1.91 us
  Pallas kernels: 6.18 us -> 5.27 us
  starting transfers between devices: 8.59 us -> 7.92 us
    unnamed x21 -> x20, local copies, waits for them, and re-layouts: 4.52 us -> 0.95 us
    ppermute x4, waiting for transfers between devices: 0.01 us -> 1.13 us  [shards(): got = [lax.ppermute(m, AXES, pairs) for m, pairs in zip(first, perms)]]
    pallas_call x5 -> x6, Pallas kernels: 6.18 us -> 5.27 us  [run(): pl.pallas_call(kernel, out_shape=outs, in_specs=[pl.BlockSpec(memory_spac...]
    ppermute x4, waiting for transfers between devices: 0.01 us -> 0.78 us  [shards(): got_more = [lax.ppermute(m, AXES, pairs) for m, pairs in zip(second, perms)]]
    ppermute x4, starting transfers between devices: 4.1 us -> 3.44 us  [shards(): got_more = [lax.ppermute(m, AXES, pairs) for m, pairs in zip(second, perms)]]
  transfers between devices with their start and end apart: 8 -> 8, of which waited for: 0 -> 2; matrix products, arithmetic and copies ran while one was open for 5% -> 0% of each run, Pallas kernels for 19% -> 23%
where the time goes in v1:
time: 16.4 us; the launch traced here: 16.2 us
  starting transfers between devices  7.92 us (48%)
  Pallas kernels  5.27 us (32%)
  waiting for transfers between devices  1.91 us (12%)
  local copies, waits for them, and re-layouts  0.95 us (6%)
    pallas_call x6, Pallas kernels, run(): pl.pallas_call(kernel, out_shape=outs, in_specs=[pl.BlockSpec(memory_spac...  5.27 us
    ppermute x4, starting transfers between devices, shards(): got = [lax.ppermute(m, AXES, pairs) for m, pairs in zip(first, perms)]  4.48 us
    ppermute x4, starting transfers between devices, shards(): got_more = [lax.ppermute(m, AXES, pairs) for m, pairs in zip(second, perms)]  3.44 us
    ppermute x4, waiting for transfers between devices, shards(): got = [lax.ppermute(m, AXES, pairs) for m, pairs in zip(first, perms)]  1.13 us
    unnamed x20, local copies, waits for them, and re-layouts  0.95 us
    ppermute x4, waiting for transfers between devices, shards(): got_more = [lax.ppermute(m, AXES, pairs) for m, pairs in zip(second, perms)]  0.78 us
  transfers between devices with their start and end apart: 8, of which 2 were waited for; matrix products, arithmetic and copies ran while one was open for 0% of the time, Pallas kernels for 23%

profile of v1, /device:TPU:0, one launch (start us, length us, event | category | flops | bytes accessed | tf_op | source)
XLA Modules:
  0.0 16.2 jit_solution(5009019257662608245)
XLA Ops:
  0.0 0.9 %copy-done.2 = bf16[128,320]{0,1:T(8,128)(2,1)S(1)} copy-done((bf16[128,320]{0,1:T(8,128)(2,1)S(1)}, bf16[128,320]{0,1:T(8,128)(2,1)}, u32[]{:S(2)}) %copy-start.2) | copy-done | bytes 81944
  0.9 0.0 copy-done.3
  0.9 0.0 copy-start.5
  1.0 0.0 copy-start.7
  1.0 0.3 %shard_map.101 = (bf16[64,128]{1,0:T(8,128)(2,1)S(1)}, bf16[16,640]{1,0:T(8,128)(2,1)S(1)}, bf16[16,640]{1,0:T(8,128)(2,1)S(1)}, bf16[16,640]{1,0:T(8,128)(2,1)S(1)}, bf16[16,640]{1,0:T(8,128)(2,1)S(1)}) custom-call(f32[64,16]{1,0:T(8,128)S(1)} %shard_map.100.mask_ref, bf16[320,128]{1,0:T(8,128)(2,1)S(1)} %bitcast.6, bf16[320,128]{1,0:T(8,128)(2,1)S(1)} %bitcast.8, ...), custom_call_target="tpu_custom_call" | custom-call | flops 1000000000 | bytes 100000 | tf_op jit(solution)/shard_map/pallas_call | solution.py:297
  1.2 0.5 %collective-permute-start = (bf16[16,640]{1,0:T(8,128)(2,1)S(1)}, bf16[16,640]{1,0:T(8,128)(2,1)S(1)}, u32[]{:S(2)}, u32[]{:S(2)}) collective-permute-start(bf16[16,640]{1,0:T(8,128)(2,1)S(1)} %get-tuple-element.30), channel_id=1, source_target_pairs={{0,4},{4,0},{8,12},{12,8},{16,20},{20,16},{24,28},{28,24},{1,5},{5... | collective-permute-start | bytes 61448 | tf_op jit(solution)/shard_map/ppermute | solution.py:320
  1.7 2.6 %collective-permute-start.1 = (bf16[16,640]{1,0:T(8,128)(2,1)S(1)}, bf16[16,640]{1,0:T(8,128)(2,1)S(1)}, u32[]{:S(2)}, u32[]{:S(2)}) collective-permute-start(bf16[16,640]{1,0:T(8,128)(2,1)S(1)} %get-tuple-element.31), channel_id=1, source_target_pairs={{4,8},{8,4},{12,16},{16,12},{20,24},{24,20},{5,9},{9,5},{13,17},{1... | collective-permute-start | bytes 61448 | tf_op jit(solution)/shard_map/ppermute | solution.py:320
  4.3 0.1 collective-permute-start.2
  4.4 1.3 %collective-permute-start.3 = (bf16[16,640]{1,0:T(8,128)(2,1)S(1)}, bf16[16,640]{1,0:T(8,128)(2,1)S(1)}, u32[]{:S(2)}, u32[]{:S(2)}) collective-permute-start(bf16[16,640]{1,0:T(8,128)(2,1)S(1)} %get-tuple-element.33), channel_id=1, source_target_pairs={{1,2},{2,1},{5,6},{6,5},{9,10},{10,9},{13,14},{14,13},{17,18},{18,... | collective-permute-start | bytes 61448 | tf_op jit(solution)/shard_map/ppermute | solution.py:320
  5.7 0.0 copy-start.6
  5.7 0.0 copy-start.9
  5.7 1.2 %shard_map.102 = (f32[128,1280]{1,0:T(8,128)S(1)}, f32[64,640]{1,0:T(8,128)S(1)}, bf16[64,512]{1,0:T(8,128)(2,1)S(1)}, bf16[256,64]{1,0:T(8,128)(2,1)S(1)}, bf16...) custom-call(bf16[320,128]{1,0:T(8,128)(2,1)S(1)} %bitcast.7, ...), custom_call_target="tpu_custom_call" | custom-call | flops 1000000000 | bytes 1000000 | tf_op jit(solution)/shard_map/pallas_call | solution.py:297
  6.9 0.0 collective-permute-done.a_ref
  6.9 0.0 collective-permute-done.1.b_ref
  6.9 1.1 %collective-permute-done.2.c_ref = bf16[16,640]{1,0:T(8,128)(2,1)S(1)} collective-permute-done((bf16[16,640]{1,0:T(8,128)(2,1)S(1)}, bf16[16,640]{1,0:T(8,128)(2,1)S(1)}, u32[]{:S(2)}, u32[]{:S(2)}) %collective-permute-start.2) | collective-permute-done | bytes 20512 | tf_op jit(solution)/shard_map/ppermute | solution.py:320
  8.1 0.0 collective-permute-done.3.d_ref
  8.1 0.4 %shard_map.104 = (bf16[16,640]{1,0:T(8,128)(2,1)S(1)}, bf16[16,640]{1,0:T(8,128)(2,1)S(1)}, bf16[16,640]{1,0:T(8,128)(2,1)S(1)}, bf16[16,640]{1,0:T(8,128)(2,1)S(1)}) custom-call(f32[64,640]{1,0:T(8,128)S(1)} %get-tuple-element.36.near_ref, bf16[256,64]{1,0:T(8,128)(2,1)S(1)} %get-tuple-element.37.hot_ref, bf16[512,256]{1,0:T(8,128)(2,1)S(1)} %get-tuple-element.38.recon_ref, ...), custom_call_target="tpu_custom_call" | custom-call | flops 1000000 | bytes 100000 | tf_op jit(solution)/shard_map/pallas_call | solution.py:297
  8.4 0.1 collective-permute-start.4
  8.5 3.0 %collective-permute-start.5 = (bf16[16,640]{1,0:T(8,128)(2,1)S(1)}, bf16[16,640]{1,0:T(8,128)(2,1)S(1)}, u32[]{:S(2)}, u32[]{:S(2)}) collective-permute-start(bf16[16,640]{1,0:T(8,128)(2,1)S(1)} %get-tuple-element.40), channel_id=1, source_target_pairs={{4,8},{8,4},{12,16},{16,12},{20,24},{24,20},{5,9},{9,5},{13,17},{1... | collective-permute-start | bytes 61448 | tf_op jit(solution)/shard_map/ppermute | solution.py:344
  11.5 0.1 collective-permute-start.6
  11.6 0.3 %collective-permute-start.7 = (bf16[16,640]{1,0:T(8,128)(2,1)S(1)}, bf16[16,640]{1,0:T(8,128)(2,1)S(1)}, u32[]{:S(2)}, u32[]{:S(2)}) collective-permute-start(bf16[16,640]{1,0:T(8,128)(2,1)S(1)} %get-tuple-element.42), channel_id=1, source_target_pairs={{1,2},{2,1},{5,6},{6,5},{9,10},{10,9},{13,14},{14,13},{17,18},{18,... | collective-permute-start | bytes 61448 | tf_op jit(solution)/shard_map/ppermute | solution.py:344
  11.9 2.6 %shard_map.103 = (f32[8,128]{1,0:T(8,128)S(1)}, f32[4,640,128]{2,1,0:T(8,128)S(1)}) custom-call(f32[128,1280]{1,0:T(8,128)S(1)} %get-tuple-element.25.near_ref, bf16[64,512]{1,0:T(8,128)(2,1)S(1)} %get-tuple-element.26.hot_ref, bf16[128,256]{1,0:T(8,128)(2,1)S(1)} %get-tuple-element.27.recon_ref, s32[6,128]{1,0:T(8,128)S(1)} %bitcast.13, ...), custom_call_target="tpu_custom_call" | custom-call | flops 1000000000 | bytes 1000000 | tf_op jit(solution)/shard_map/pallas_call | solution.py:297
  14.5 0.8 %collective-permute-done.6.c_ref = bf16[16,640]{1,0:T(8,128)(2,1)S(1)} collective-permute-done((bf16[16,640]{1,0:T(8,128)(2,1)S(1)}, bf16[16,640]{1,0:T(8,128)(2,1)S(1)}, u32[]{:S(2)}, u32[]{:S(2)}) %collective-permute-start.6) | collective-permute-done | bytes 20512 | tf_op jit(solution)/shard_map/ppermute | solution.py:344
  15.3 0.9 %shard_map.105 = f32[1,128]{1,0:T(1,128)} custom-call(f32[8,128]{1,0:T(8,128)S(1)} %get-tuple-element.34.part_ref, f32[4,640,128]{2,1,0:T(8,128)S(1)} %get-tuple-element.35.coef_ref, bf16[64,512]{1,0:T(8,128)(2,1)S(1)} %get-tuple-element.26.hot_ref, bf16[16,640]{1,0:T(8,128)(2,1)S(1)} %collective-permute-done.4.a_ref, ...), custom_call_target="tpu_custom_call" | custom-call | flops 1000000 | bytes 100000 | tf_op jit(solution)/shard_map/pallas_call | solution.py:297
  (18 shorter events, 0.0 us)
Async XLA Ops:
  0.0 0.9 %copy-start.2 = (bf16[128,320]{0,1:T(8,128)(2,1)S(1)}, bf16[128,320]{0,1:T(8,128)(2,1)}, u32[]{:S(2)}) copy-start(bf16[128,320]{0,1:T(8,128)(2,1)} %param.10) | copy-start | bytes 245764
  0.0 0.9 %copy-start.3 = (bf16[128,320]{0,1:T(8,128)(2,1)S(1)}, bf16[128,320]{0,1:T(8,128)(2,1)}, u32[]{:S(2)}) copy-start(bf16[128,320]{0,1:T(8,128)(2,1)} %param.11) | copy-start | bytes 245764
  0.0 0.9 %copy-start.8 = (s32[4,16]{1,0:T(4,128)S(1)}, s32[4,16]{1,0:T(4,128)}, u32[]{:S(2)}) copy-start(s32[4,16]{1,0:T(4,128)} %send_ref.1) | copy-start | bytes 772
  0.9 4.8 %copy-start = (bf16[7,64,125]{2,1,0:T(8,128)(2,1)S(1)}, bf16[7,64,125]{2,1,0:T(8,128)(2,1)}, u32[]{:S(2)}) copy-start(bf16[7,64,125]{2,1,0:T(8,128)(2,1)} %recon_ref.1) | copy-start | bytes 336004
  0.9 4.8 %copy-start.1 = (bf16[3,125,125]{2,1,0:T(8,128)(2,1)S(1)}, bf16[3,125,125]{2,1,0:T(8,128)(2,1)}, u32[]{:S(2)}) copy-start(bf16[3,125,125]{2,1,0:T(8,128)(2,1)} %deriv_ref.1) | copy-start | bytes 281254
  0.9 4.8 %copy-start.4 = (bf16[150,125]{1,0:T(8,128)(2,1)S(1)}, bf16[150,125]{1,0:T(8,128)(2,1)}, u32[]{:S(2)}) copy-start(bf16[150,125]{1,0:T(8,128)(2,1)} %lift_ref.1) | copy-start | bytes 112504
  0.9 4.8 %copy-start.5 = (bf16[125,150]{0,1:T(8,128)(2,1)S(1)}, bf16[125,150]{0,1:T(8,128)(2,1)}, u32[]{:S(2)}) copy-start(bf16[125,150]{0,1:T(8,128)(2,1)} %param.17) | copy-start | bytes 112504
  1.0 4.8 %copy-start.7 = (s32[128,6]{0,1:T(8,128)S(1)}, s32[128,6]{0,1:T(8,128)}, u32[]{:S(2)}) copy-start(s32[128,6]{0,1:T(8,128)} %param.13) | copy-start | bytes 9220
  1.2 5.7 %collective-permute-start = (bf16[16,640]{1,0:T(8,128)(2,1)S(1)}, bf16[16,640]{1,0:T(8,128)(2,1)S(1)}, u32[]{:S(2)}, u32[]{:S(2)}) collective-permute-start(bf16[16,640]{1,0:T(8,128)(2,1)S(1)} %get-tuple-element.30), channel_id=1, source_target_pairs={{0,4},{4,0},{8,12},{12,8},{16,20},{20,16},{24,28},{28,24},{1,5},{5... | collective-permute-start | bytes 61448 | tf_op jit(solution)/shard_map/ppermute | solution.py:320
  1.7 5.2 %collective-permute-start.1 = (bf16[16,640]{1,0:T(8,128)(2,1)S(1)}, bf16[16,640]{1,0:T(8,128)(2,1)S(1)}, u32[]{:S(2)}, u32[]{:S(2)}) collective-permute-start(bf16[16,640]{1,0:T(8,128)(2,1)S(1)} %get-tuple-element.31), channel_id=1, source_target_pairs={{4,8},{8,4},{12,16},{16,12},{20,24},{24,20},{5,9},{9,5},{13,17},{1... | collective-permute-start | bytes 61448 | tf_op jit(solution)/shard_map/ppermute | solution.py:320
  4.3 3.8 %collective-permute-start.2 = (bf16[16,640]{1,0:T(8,128)(2,1)S(1)}, bf16[16,640]{1,0:T(8,128)(2,1)S(1)}, u32[]{:S(2)}, u32[]{:S(2)}) collective-permute-start(bf16[16,640]{1,0:T(8,128)(2,1)S(1)} %get-tuple-element.32), channel_id=1, source_target_pairs={{0,1},{1,0},{2,3},{3,2},{4,5},{5,4},{6,7},{7,6},{8,9},{9,8},{10,11... | collective-permute-start | bytes 61448 | tf_op jit(solution)/shard_map/ppermute | solution.py:320
  4.4 3.7 %collective-permute-start.3 = (bf16[16,640]{1,0:T(8,128)(2,1)S(1)}, bf16[16,640]{1,0:T(8,128)(2,1)S(1)}, u32[]{:S(2)}, u32[]{:S(2)}) collective-permute-start(bf16[16,640]{1,0:T(8,128)(2,1)S(1)} %get-tuple-element.33), channel_id=1, source_target_pairs={{1,2},{2,1},{5,6},{6,5},{9,10},{10,9},{13,14},{14,13},{17,18},{18,... | collective-permute-start | bytes 61448 | tf_op jit(solution)/shard_map/ppermute | solution.py:320
  5.7 6.2 %copy-start.6 = (f32[3,5,5]{2,0,1:T(4,128)S(1)}, f32[3,5,5]{2,0,1:T(4,128)}, u32[]{:S(2)}) copy-start(f32[3,5,5]{2,0,1:T(4,128)} %param.16) | copy-start | bytes 904
  5.7 6.2 %copy-start.9 = (f32[5]{0:T(128)S(1)}, f32[5]{0:T(128)}, u32[]{:S(2)}) copy-start(f32[5]{0:T(128)} %dissip_ref.1) | copy-start | bytes 64
  8.4 6.1 %collective-permute-start.4 = (bf16[16,640]{1,0:T(8,128)(2,1)S(1)}, bf16[16,640]{1,0:T(8,128)(2,1)S(1)}, u32[]{:S(2)}, u32[]{:S(2)}) collective-permute-start(bf16[16,640]{1,0:T(8,128)(2,1)S(1)} %get-tuple-element.39), channel_id=1, source_target_pairs={{0,4},{4,0},{8,12},{12,8},{16,20},{20,16},{24,28},{28,24},{1,5},{5... | collective-permute-start | bytes 61448 | tf_op jit(solution)/shard_map/ppermute | solution.py:344
  8.5 6.0 %collective-permute-start.5 = (bf16[16,640]{1,0:T(8,128)(2,1)S(1)}, bf16[16,640]{1,0:T(8,128)(2,1)S(1)}, u32[]{:S(2)}, u32[]{:S(2)}) collective-permute-start(bf16[16,640]{1,0:T(8,128)(2,1)S(1)} %get-tuple-element.40), channel_id=1, source_target_pairs={{4,8},{8,4},{12,16},{16,12},{20,24},{24,20},{5,9},{9,5},{13,17},{1... | collective-permute-start | bytes 61448 | tf_op jit(solution)/shard_map/ppermute | solution.py:344
  11.5 3.8 %collective-permute-start.6 = (bf16[16,640]{1,0:T(8,128)(2,1)S(1)}, bf16[16,640]{1,0:T(8,128)(2,1)S(1)}, u32[]{:S(2)}, u32[]{:S(2)}) collective-permute-start(bf16[16,640]{1,0:T(8,128)(2,1)S(1)} %get-tuple-element.41), channel_id=1, source_target_pairs={{0,1},{1,0},{2,3},{3,2},{4,5},{5,4},{6,7},{7,6},{8,9},{9,8},{10,11... | collective-permute-start | bytes 61448 | tf_op jit(solution)/shard_map/ppermute | solution.py:344
  11.6 3.7 %collective-permute-start.7 = (bf16[16,640]{1,0:T(8,128)(2,1)S(1)}, bf16[16,640]{1,0:T(8,128)(2,1)S(1)}, u32[]{:S(2)}, u32[]{:S(2)}) collective-permute-start(bf16[16,640]{1,0:T(8,128)(2,1)S(1)} %get-tuple-element.42), channel_id=1, source_target_pairs={{1,2},{2,1},{5,6},{6,5},{9,10},{10,9},{13,14},{14,13},{17,18},{18,... | collective-permute-start | bytes 61448 | tf_op jit(solution)/shard_map/ppermute | solution.py:344

commit v2 on v1

--- a/solution.py
+++ b/solution.py
@@ -47,13 +47,13 @@
     for j in {0, ny - 1 if ny % 2 == 0 else 0}:
         for i in range(0, nx - 1, 2):
             y_odd += both(joint(i, j), joint(i + 1, j))
-    return x_even, x_odd, y_even, y_odd
+    return y_even, y_odd, x_odd, x_even
 
 
 def directions():
     odd_x = lax.rem(lax.axis_index("rx"), 2)
     odd_y = lax.rem(lax.axis_index("ry"), 2)
-    return 1 - odd_x, odd_x, 3 - odd_y, 2 + odd_y
+    return 3 - odd_y, 2 + odd_y, odd_x, 1 - odd_x
 
 
 def iota(shape, dim):
@@ -112,14 +112,19 @@
     lift_ref,
     trace_ref,
     pick_ref,
+    jacob_ref,
+    dissip_ref,
     near_ref,
     listed_ref,
     hot_ref,
     listed_hot_ref,
     far_recon_ref,
     pair_recon_ref,
-    weights_ref,
+    inner_ref,
+    pairs_ref,
     back_ref,
+    local_ref,
+    factors_ref,
     gathered_ref,
     tall_ref,
     square_ref,
@@ -154,6 +159,7 @@
     local = jnp.concatenate(
         [hot(iota((count, count), 0), nbr_ref[f : f + 1, :]).astype(BF16) for f in range(FACES)], axis=1
     )
+    local_ref[...] = local
     for i, ref in enumerate((primal_ref, adjoint_ref)):
         state = ref[...]
         found = dot(state, local).astype(BF16)
@@ -184,22 +190,24 @@
     for f in range(FACES):
         blocks.append(jnp.where(face == f ^ 1, down if f % 2 else up, 0.0) * 0.5)
     products = dot(jnp.concatenate(blocks, axis=0).astype(BF16), trace_pad_ref[...])
-    weights_ref[...] = jnp.zeros_like(weights_ref)
     square_ref[...] = jnp.zeros_like(square_ref)
     for a in range(3):
         square_ref[0:ENR, 0:ENR] = deriv_ref[a].astype(F32)
-        weights_ref[a * LANE : (a + 1) * LANE, 0:LANE] = (
-            square_ref[...].T + products[a * LANE : (a + 1) * LANE]
-        ).astype(BF16)
-    weights_ref[3 * LANE : 4 * LANE, 0:LANE] = products[3 * LANE : 4 * LANE].astype(BF16)
+        inner_ref[a * LANE : (a + 1) * LANE, :] = (square_ref[...].T + rows(products, a)).astype(BF16)
+    inner_ref[3 * LANE :, :] = rows(products, 3).astype(BF16)
     for f in range(FACES):
-        across = products[(4 + f) * LANE : (5 + f) * LANE]
-        place = slice((f + 1) * LANE, (f + 2) * LANE)
-        row = (f // 2) * LANE
-        weights_ref[row : row + LANE, place] = (-across if f % 2 else across).astype(BF16)
-        weights_ref[3 * LANE : 4 * LANE, place] = across.astype(BF16)
+        across = rows(products, 4 + f)
+        place = slice((f % 2) * LANE, (f % 2 + 1) * LANE)
+        pairs_ref[f // 2, 0:LANE, place] = (-across if f % 2 else across).astype(BF16)
+        pairs_ref[f // 2, LANE:, place] = across.astype(BF16)
         if f < 4:
             back_ref[f] = across.T.astype(BF16)
+    for w in range(VARS):
+        for v in range(VARS):
+            at = (w * VARS + v) * 3
+            factors_ref[at : at + 3, :] = jnp.broadcast_to(jacob_ref[v][:, w : w + 1], (3, count))
+        at = 15 * VARS + w
+        factors_ref[at : at + 1, :] = jnp.broadcast_to(dissip_ref[:, w : w + 1], (1, count))
 
 
 def listed_kernel(near_ref, hot_ref, recon_ref, a_ref, b_ref, c_ref, d_ref, *messages):
@@ -220,11 +228,11 @@
     near_ref,
     hot_ref,
     recon_ref,
-    nbr_ref,
-    weights_ref,
+    local_ref,
+    inner_ref,
+    pairs_ref,
     back_ref,
-    jacob_ref,
-    dissip_ref,
+    factors_ref,
     a_ref,
     b_ref,
     c_ref,
@@ -235,7 +243,7 @@
     state_ref,
     signed_ref,
 ):
-    count = nbr_ref.shape[1]
+    count = local_ref.shape[0]
     packed = jnp.concatenate([ref[...] for ref in (a_ref, b_ref, c_ref, d_ref)], axis=0)
     found = dot_rows(packed, hot_ref[...]).astype(BF16)
     far = [
@@ -250,45 +258,52 @@
     ]
     u = (near_ref[:, 0:WIDE] + dot(recon_ref[...], far[0])).astype(BF16)
     state_ref[...] = near_ref[:, WIDE:] + dot(recon_ref[...], far[1])
-    right_ref[0:LANE, :] = u
     stack = jnp.concatenate([lanes(u, v) for v in range(VARS)], axis=0)
-    local = jnp.concatenate(
-        [hot(iota((count, count), 0), nbr_ref[f : f + 1, :]).astype(BF16) for f in range(FACES)], axis=1
-    )
-    across = dot(stack, local).astype(BF16)
+    across = dot(stack, local_ref[...]).astype(BF16)
     for f in range(FACES):
         for v in range(VARS):
-            right_ref[(f + 1) * LANE : (f + 2) * LANE, v * count : (v + 1) * count] = rows(lanes(across, f), v)
-    mixed = dot(weights_ref[...], right_ref[...])
-    part = jnp.zeros((LANE, count), F32)
-    for w in range(VARS):
-        place = slice(w * count, (w + 1) * count)
-        damped = dissip_ref[w] * state_ref[:, place]
-        part = part + damped * mixed[3 * LANE :, place]
-        for a in range(3):
-            turned = jacob_ref[0, a, w] * state_ref[:, 0:count]
-            for v in range(1, VARS):
-                turned = turned + jacob_ref[v, a, w] * state_ref[:, v * count : (v + 1) * count]
-            part = part + turned * mixed[a * LANE : (a + 1) * LANE, place]
-            if a < 2:
-                signed_ref[2 * a, :, place] = (damped + turned).astype(BF16)
-                signed_ref[2 * a + 1, :, place] = (damped - turned).astype(BF16)
-    for f in range(4):
-        coef = dot(back_ref[f], signed_ref[f])
+            right_ref[f * LANE : (f + 1) * LANE, v * count : (v + 1) * count] = rows(lanes(across, f), v)
+    mixed = dot(inner_ref[...], u)
+    turns = [dot(pairs_ref[a], right_ref[2 * a * LANE : 2 * (a + 1) * LANE, :]) for a in range(3)]
+    total = jnp.zeros((8, count), F32)
+    height = 32
+    for c in range(LANE // height):
+        at = slice(c * height, (c + 1) * height)
+        low = slice(LANE + c * height, LANE + (c + 1) * height)
+        z = [state_ref[at, v * count : (v + 1) * count] for v in range(VARS)]
+        part = jnp.zeros((height, count), F32)
+        for w in range(VARS):
+            place = slice(w * count, (w + 1) * count)
+            damped = factors_ref[15 * VARS + w : 15 * VARS + w + 1, :] * z[w]
+            bottom = slice(3 * LANE + c * height, 3 * LANE + (c + 1) * height)
+            whole = mixed[bottom, place] + turns[0][low, place] + turns[1][low, place] + turns[2][low, place]
+            part = part + damped * whole
+            for a in range(3):
+                row = w * VARS * 3 + a
+                turned = factors_ref[row : row + 1, :] * z[0]
+                for v in range(1, VARS):
+                    turned = turned + factors_ref[row + 3 * v : row + 3 * v + 1, :] * z[v]
+                side = slice(a * LANE + c * height, a * LANE + (c + 1) * height)
+                part = part + turned * (mixed[side, place] + turns[a][at, place])
+                if a < 2:
+                    signed_ref[2 * a, at, place] = (damped + turned).astype(BF16)
+                    signed_ref[2 * a + 1, at, place] = (damped - turned).astype(BF16)
+        total = total + jnp.sum(part.reshape(height // 8, 8, count), axis=0)
+    for j, face in enumerate(directions()):
+        coef = dot(back_ref[face], signed_ref[face]).astype(BF16)
         for v in range(VARS):
-            coef_ref[f, v * LANE : (v + 1) * LANE, :] = lanes(coef, v)
-    part_ref[...] = jnp.sum(part.reshape(LANE // 8, 8, count), axis=0)
+            coef_ref[v * LANE : (v + 1) * LANE, j * count : (j + 1) * count] = lanes(coef, v)
+    part_ref[...] = total
 
 
 def last_kernel(part_ref, coef_ref, hot_ref, a_ref, b_ref, c_ref, d_ref, out_ref):
     packed = jnp.concatenate([ref[...] for ref in (a_ref, b_ref, c_ref, d_ref)], axis=0)
-    found = dot_rows(packed, hot_ref[...])
-    terms = lanes(found, 0) * coef_ref[directions()[0]]
-    for j, face in enumerate(directions()):
-        if j:
-            terms = terms + lanes(found, j) * coef_ref[face]
-    total = part_ref[...] + jnp.sum(terms.reshape(WIDE // 8, 8, terms.shape[1]), axis=0)
-    out_ref[...] = 0.04 * jnp.sum(total, axis=0, keepdims=True)
+    terms = dot(packed, coef_ref[...]) * hot_ref[...].astype(F32)
+    sums = jnp.sum(terms, axis=0, keepdims=True)
+    total = jnp.sum(part_ref[...], axis=0, keepdims=True)
+    for j in range(4):
+        total = total + lanes(sums, j)
+    out_ref[...] = 0.04 * total
 
 
 def call(kernel, outs, specs=None, scratch=(), flops=10**6, moved=10**5, grant=VMEM_BYTES):
@@ -318,7 +333,7 @@
         mask, primal_t, adjoint_t, send_index
     )
     got = [lax.ppermute(m, AXES, pairs) for m, pairs in zip(first, perms)]
-    near, listed, hots, listed_hots, far_recon, pair_recon, weights, back = call(
+    near, listed, hots, listed_hots, far_recon, pair_recon, inner, pairs, back, local, factors = call(
         local_kernel,
         [
             shape((LANE, 2 * WIDE), F32),
@@ -327,8 +342,11 @@
             shape((16 * sent, 4 * sent), BF16),
             shape((LANE, 4 * MODES), BF16),
             shape((4 * LANE, 2 * LANE), BF16),
-            shape((4 * LANE, 7 * LANE), BF16),
+            shape((4 * LANE, LANE), BF16),
+            shape((3, 2 * LANE, 2 * LANE), BF16),
             shape((4, LANE, LANE), BF16),
+            shape((count, FACES * count), BF16),
+            shape((16 * VARS, count), F32),
         ],
         scratch=[
             vmem((PATCH * MODES, 2 * WIDE), BF16),
@@ -337,19 +355,18 @@
             vmem((2 * LANE, LANE), F32),
             vmem((2 * LANE, LANE), BF16),
         ],
-        flops=10**9,
+        flops=3 * 10**9,
         moved=10**6,
-    )(primal_t, adjoint_t, nbr, recon, deriv, lift, face_trace.T, pick)
+    )(primal_t, adjoint_t, nbr, recon, deriv, lift, face_trace.T, pick, jacob.transpose(1, 0, 2), dissip[None])
     second = call(listed_kernel, [message] * 4)(listed, listed_hots, pair_recon, *got)
     got_more = [lax.ppermute(m, AXES, pairs) for m, pairs in zip(second, perms)]
     part, coef = call(
         middle_kernel,
-        [shape((8, count), F32), shape((4, WIDE, count), F32)],
-        specs=[vmem] * 6 + [smem] * 2 + [vmem] * 4,
-        scratch=[vmem((7 * LANE, WIDE), BF16), vmem((LANE, WIDE), F32), vmem((4, LANE, WIDE), BF16)],
+        [shape((8, count), F32), shape((WIDE, 4 * count), BF16)],
+        scratch=[vmem((FACES * LANE, WIDE), BF16), vmem((LANE, WIDE), F32), vmem((4, LANE, WIDE), BF16)],
         flops=10**9,
         moved=10**6,
-    )(near, hots, far_recon, nbr, weights, back, jacob.transpose(1, 0, 2), dissip, *got)
+    )(near, hots, far_recon, local, inner, pairs, back, factors, *got)
     out = call(last_kernel, shape((1, count), F32))(part, coef, hots, *got_more)
     return out.reshape(count)
 

time: 16.4 us -> 16.1 us (0.982)
  starting transfers between devices: 7.92 us -> 9.32 us
  Pallas kernels: 5.27 us -> 4.13 us
  waiting for transfers between devices: 1.91 us -> 0.82 us
  local copies, waits for them, and re-layouts: 0.95 us -> 1.57 us
    ppermute x4, starting transfers between devices: 4.48 us -> 5.98 us  [shards(): got = [lax.ppermute(m, AXES, pairs) for m, pairs in zip(first, perms)]]
    pallas_call x6, Pallas kernels: 5.27 us -> 4.13 us  [run(): pl.pallas_call(kernel, out_shape=outs, in_specs=[pl.BlockSpec(memory_spac...]
    ppermute x4, waiting for transfers between devices: 1.13 us -> 0.13 us  [shards(): got = [lax.ppermute(m, AXES, pairs) for m, pairs in zip(first, perms)]]
    unnamed x20, local copies, waits for them, and re-layouts: 0.95 us -> 1.57 us
  transfers between devices with their start and end apart: 8 -> 8, of which waited for: 2 -> 2; matrix products, arithmetic and copies ran while one was open for 0% -> 0% of each run, Pallas kernels for 23% -> 17%
where the time goes in v2:
time: 16.1 us; the launch traced here: 15.9 us
  starting transfers between devices  9.32 us (58%)
  Pallas kernels  4.13 us (26%)
  local copies, waits for them, and re-layouts  1.57 us (10%)
  waiting for transfers between devices  0.82 us (5%)
    ppermute x4, starting transfers between devices, shards(): got = [lax.ppermute(m, AXES, pairs) for m, pairs in zip(first, perms)]  5.98 us
    pallas_call x6, Pallas kernels, run(): pl.pallas_call(kernel, out_shape=outs, in_specs=[pl.BlockSpec(memory_spac...  4.13 us
    ppermute x4, starting transfers between devices, shards(): got_more = [lax.ppermute(m, AXES, pairs) for m, pairs in zip(second, perms)]  3.34 us
    unnamed x20, local copies, waits for them, and re-layouts  1.57 us
    ppermute x4, waiting for transfers between devices, shards(): got_more = [lax.ppermute(m, AXES, pairs) for m, pairs in zip(second, perms)]  0.68 us
  transfers between devices with their start and end apart: 8, of which 2 were waited for; matrix products, arithmetic and copies ran while one was open for 0% of the time, Pallas kernels for 17%

profile of v2, /device:TPU:0, one launch (start us, length us, event | category | flops | bytes accessed | tf_op | source)
XLA Modules:
  0.0 15.9 jit_solution(15717577434950910291)
XLA Ops:
  0.0 0.0 copy-start.8
  0.0 0.9 %copy-done.2 = bf16[128,320]{0,1:T(8,128)(2,1)S(1)} copy-done((bf16[128,320]{0,1:T(8,128)(2,1)S(1)}, bf16[128,320]{0,1:T(8,128)(2,1)}, u32[]{:S(2)}) %copy-start.2) | copy-done | bytes 81944
  0.9 0.0 copy-done.3
  0.9 0.0 copy-start.5
  1.0 0.3 %shard_map.101 = (bf16[64,128]{1,0:T(8,128)(2,1)S(1)}, bf16[16,640]{1,0:T(8,128)(2,1)S(1)}, bf16[16,640]{1,0:T(8,128)(2,1)S(1)}, bf16[16,640]{1,0:T(8,128)(2,1)S(1)}, bf16[16,640]{1,0:T(8,128)(2,1)S(1)}) custom-call(f32[64,16]{1,0:T(8,128)S(1)} %shard_map.100.mask_ref, bf16[320,128]{1,0:T(8,128)(2,1)S(1)} %bitcast.7, bf16[320,128]{1,0:T(8,128)(2,1)S(1)} %bitcast.9, ...), custom_call_target="tpu_custom_call" | custom-call | flops 1000000000 | bytes 100000 | tf_op jit(solution)/shard_map/pallas_call | solution.py:312
  1.2 3.0 %collective-permute-start = (bf16[16,640]{1,0:T(8,128)(2,1)S(1)}, bf16[16,640]{1,0:T(8,128)(2,1)S(1)}, u32[]{:S(2)}, u32[]{:S(2)}) collective-permute-start(bf16[16,640]{1,0:T(8,128)(2,1)S(1)} %get-tuple-element.36), channel_id=1, source_target_pairs={{0,1},{1,0},{2,3},{3,2},{4,5},{5,4},{6,7},{7,6},{8,9},{9,8},{10,11... | collective-permute-start | bytes 61448 | tf_op jit(solution)/shard_map/ppermute | solution.py:335
  4.2 0.0 collective-permute-start.1
  4.2 3.0 %collective-permute-start.2 = (bf16[16,640]{1,0:T(8,128)(2,1)S(1)}, bf16[16,640]{1,0:T(8,128)(2,1)S(1)}, u32[]{:S(2)}, u32[]{:S(2)}) collective-permute-start(bf16[16,640]{1,0:T(8,128)(2,1)S(1)} %get-tuple-element.38), channel_id=1, source_target_pairs={{4,8},{8,4},{12,16},{16,12},{20,24},{24,20},{5,9},{9,5},{13,17},{1... | collective-permute-start | bytes 61448 | tf_op jit(solution)/shard_map/ppermute | solution.py:335
  7.2 0.0 collective-permute-start.3
  7.2 0.6 %copy-done.7 = s32[128,6]{0,1:T(8,128)S(1)} copy-done((s32[128,6]{0,1:T(8,128)S(1)}, s32[128,6]{0,1:T(8,128)}, u32[]{:S(2)}) %copy-start.7) | copy-done | bytes 3096
  7.9 1.1 %shard_map.102 = (f32[128,1280]{1,0:T(8,128)S(1)}, f32[64,640]{1,0:T(8,128)S(1)}, bf16[64,512]{1,0:T(8,128)(2,1)S(1)}, bf16[256,64]{1,0:T(8,128)(2,1)S(1)}, bf16...) custom-call(bf16[320,128]{1,0:T(8,128)(2,1)S(1)} %bitcast.8, ...), custom_call_target="tpu_custom_call" | custom-call | flops 3000000000 | bytes 1000000 | tf_op jit(solution)/shard_map/pallas_call | solution.py:312
  9.0 0.0 collective-permute-done.a_ref
  9.0 0.0 collective-permute-done.1.b_ref
  9.0 0.1 collective-permute-done.2.c_ref
  9.2 0.0 collective-permute-done.3.d_ref
  9.2 0.4 %shard_map.104 = (bf16[16,640]{1,0:T(8,128)(2,1)S(1)}, bf16[16,640]{1,0:T(8,128)(2,1)S(1)}, bf16[16,640]{1,0:T(8,128)(2,1)S(1)}, bf16[16,640]{1,0:T(8,128)(2,1)S(1)}) custom-call(f32[64,640]{1,0:T(8,128)S(1)} %get-tuple-element.42.near_ref, bf16[256,64]{1,0:T(8,128)(2,1)S(1)} %get-tuple-element.43.hot_ref, bf16[512,256]{1,0:T(8,128)(2,1)S(1)} %get-tuple-element.44.recon_ref, ...), custom_call_target="tpu_custom_call" | custom-call | flops 1000000 | bytes 100000 | tf_op jit(solution)/shard_map/pallas_call | solution.py:312
  9.5 1.9 %collective-permute-start.4 = (bf16[16,640]{1,0:T(8,128)(2,1)S(1)}, bf16[16,640]{1,0:T(8,128)(2,1)S(1)}, u32[]{:S(2)}, u32[]{:S(2)}) collective-permute-start(bf16[16,640]{1,0:T(8,128)(2,1)S(1)} %get-tuple-element.45), channel_id=1, source_target_pairs={{0,1},{1,0},{2,3},{3,2},{4,5},{5,4},{6,7},{7,6},{8,9},{9,8},{10,11... | collective-permute-start | bytes 61448 | tf_op jit(solution)/shard_map/ppermute | solution.py:362
  11.4 1.0 %collective-permute-start.6 = (bf16[16,640]{1,0:T(8,128)(2,1)S(1)}, bf16[16,640]{1,0:T(8,128)(2,1)S(1)}, u32[]{:S(2)}, u32[]{:S(2)}) collective-permute-start(bf16[16,640]{1,0:T(8,128)(2,1)S(1)} %get-tuple-element.47), channel_id=1, source_target_pairs={{4,8},{8,4},{12,16},{16,12},{20,24},{24,20},{5,9},{9,5},{13,17},{1... | collective-permute-start | bytes 61448 | tf_op jit(solution)/shard_map/ppermute | solution.py:362
  12.4 0.5 %collective-permute-start.7 = (bf16[16,640]{1,0:T(8,128)(2,1)S(1)}, bf16[16,640]{1,0:T(8,128)(2,1)S(1)}, u32[]{:S(2)}, u32[]{:S(2)}) collective-permute-start(bf16[16,640]{1,0:T(8,128)(2,1)S(1)} %get-tuple-element.48), channel_id=1, source_target_pairs={{0,4},{4,0},{8,12},{12,8},{16,20},{20,16},{24,28},{28,24},{1,5},{5... | collective-permute-start | bytes 61448 | tf_op jit(solution)/shard_map/ppermute | solution.py:362
  12.9 1.6 %shard_map.103 = (f32[8,128]{1,0:T(8,128)S(1)}, bf16[640,512]{1,0:T(8,128)(2,1)S(1)}) custom-call(f32[128,1280]{1,0:T(8,128)S(1)} %get-tuple-element.28.near_ref, bf16[64,512]{1,0:T(8,128)(2,1)S(1)} %get-tuple-element.29.hot_ref, bf16[128,256]{1,0:T(8,128)(2,1)S(1)} %get-tuple-element.30.recon_ref, bf16[128,768]{1,0:T(8,128)(2,1)S(1)} %get-tuple-element.31.local_ref, ...), custom_call_target="tpu_custom_call" | custom-call | flops 1000000000 | bytes 1000000 | tf_op jit(solution)/shard_map/pallas_call | solution.py:312
  14.5 0.0 collective-permute-done.4.a_ref
  14.5 0.7 %collective-permute-done.6.c_ref = bf16[16,640]{1,0:T(8,128)(2,1)S(1)} collective-permute-done((bf16[16,640]{1,0:T(8,128)(2,1)S(1)}, bf16[16,640]{1,0:T(8,128)(2,1)S(1)}, u32[]{:S(2)}, u32[]{:S(2)}) %collective-permute-start.6) | collective-permute-done | bytes 20512 | tf_op jit(solution)/shard_map/ppermute | solution.py:362
  15.2 0.0 collective-permute-done.7.d_ref
  15.2 0.8 %shard_map.105 = f32[1,128]{1,0:T(1,128)} custom-call(f32[8,128]{1,0:T(8,128)S(1)} %get-tuple-element.40.part_ref, bf16[640,512]{1,0:T(8,128)(2,1)S(1)} %get-tuple-element.41.coef_ref, bf16[64,512]{1,0:T(8,128)(2,1)S(1)} %get-tuple-element.29.hot_ref, bf16[16,640]{1,0:T(8,128)(2,1)S(1)} %collective-permute-done.4.a_ref, ...), custom_call_target="tpu_custom_call" | custom-call | flops 1000000 | bytes 100000 | tf_op jit(solution)/shard_map/pallas_call | solution.py:312
  (18 shorter events, 0.0 us)
Async XLA Ops:
  0.0 0.9 %copy-start.2 = (bf16[128,320]{0,1:T(8,128)(2,1)S(1)}, bf16[128,320]{0,1:T(8,128)(2,1)}, u32[]{:S(2)}) copy-start(bf16[128,320]{0,1:T(8,128)(2,1)} %param.10) | copy-start | bytes 245764
  0.0 0.9 %copy-start.3 = (bf16[128,320]{0,1:T(8,128)(2,1)S(1)}, bf16[128,320]{0,1:T(8,128)(2,1)}, u32[]{:S(2)}) copy-start(bf16[128,320]{0,1:T(8,128)(2,1)} %param.11) | copy-start | bytes 245764
  0.0 0.9 %copy-start.8 = (s32[4,16]{1,0:T(4,128)S(1)}, s32[4,16]{1,0:T(4,128)}, u32[]{:S(2)}) copy-start(s32[4,16]{1,0:T(4,128)} %send_ref.1) | copy-start | bytes 772
  0.9 6.3 %copy-start = (bf16[7,64,125]{2,1,0:T(8,128)(2,1)S(1)}, bf16[7,64,125]{2,1,0:T(8,128)(2,1)}, u32[]{:S(2)}) copy-start(bf16[7,64,125]{2,1,0:T(8,128)(2,1)} %recon_ref.1) | copy-start | bytes 336004
  0.9 6.3 %copy-start.1 = (bf16[3,125,125]{2,1,0:T(8,128)(2,1)S(1)}, bf16[3,125,125]{2,1,0:T(8,128)(2,1)}, u32[]{:S(2)}) copy-start(bf16[3,125,125]{2,1,0:T(8,128)(2,1)} %deriv_ref.1) | copy-start | bytes 281254
  0.9 6.3 %copy-start.4 = (bf16[150,125]{1,0:T(8,128)(2,1)S(1)}, bf16[150,125]{1,0:T(8,128)(2,1)}, u32[]{:S(2)}) copy-start(bf16[150,125]{1,0:T(8,128)(2,1)} %lift_ref.1) | copy-start | bytes 112504
  0.9 6.3 %copy-start.5 = (bf16[125,150]{0,1:T(8,128)(2,1)S(1)}, bf16[125,150]{0,1:T(8,128)(2,1)}, u32[]{:S(2)}) copy-start(bf16[125,150]{0,1:T(8,128)(2,1)} %param.17) | copy-start | bytes 112504
  1.2 6.0 %copy-start.6 = (f32[3,5,5]{2,0,1:T(4,128)S(1)}, f32[3,5,5]{2,0,1:T(4,128)}, u32[]{:S(2)}) copy-start(f32[3,5,5]{2,0,1:T(4,128)} %param.16) | copy-start | bytes 904
  1.2 7.8 %collective-permute-start = (bf16[16,640]{1,0:T(8,128)(2,1)S(1)}, bf16[16,640]{1,0:T(8,128)(2,1)S(1)}, u32[]{:S(2)}, u32[]{:S(2)}) collective-permute-start(bf16[16,640]{1,0:T(8,128)(2,1)S(1)} %get-tuple-element.36), channel_id=1, source_target_pairs={{0,1},{1,0},{2,3},{3,2},{4,5},{5,4},{6,7},{7,6},{8,9},{9,8},{10,11... | collective-permute-start | bytes 61448 | tf_op jit(solution)/shard_map/ppermute | solution.py:335
  4.2 4.8 %collective-permute-start.1 = (bf16[16,640]{1,0:T(8,128)(2,1)S(1)}, bf16[16,640]{1,0:T(8,128)(2,1)S(1)}, u32[]{:S(2)}, u32[]{:S(2)}) collective-permute-start(bf16[16,640]{1,0:T(8,128)(2,1)S(1)} %get-tuple-element.37), channel_id=1, source_target_pairs={{1,2},{2,1},{5,6},{6,5},{9,10},{10,9},{13,14},{14,13},{17,18},{18,... | collective-permute-start | bytes 61448 | tf_op jit(solution)/shard_map/ppermute | solution.py:335
  4.2 5.0 %collective-permute-start.2 = (bf16[16,640]{1,0:T(8,128)(2,1)S(1)}, bf16[16,640]{1,0:T(8,128)(2,1)S(1)}, u32[]{:S(2)}, u32[]{:S(2)}) collective-permute-start(bf16[16,640]{1,0:T(8,128)(2,1)S(1)} %get-tuple-element.38), channel_id=1, source_target_pairs={{4,8},{8,4},{12,16},{16,12},{20,24},{24,20},{5,9},{9,5},{13,17},{1... | collective-permute-start | bytes 61448 | tf_op jit(solution)/shard_map/ppermute | solution.py:335
  7.2 2.0 %collective-permute-start.3 = (bf16[16,640]{1,0:T(8,128)(2,1)S(1)}, bf16[16,640]{1,0:T(8,128)(2,1)S(1)}, u32[]{:S(2)}, u32[]{:S(2)}) collective-permute-start(bf16[16,640]{1,0:T(8,128)(2,1)S(1)} %get-tuple-element.39), channel_id=1, source_target_pairs={{0,4},{4,0},{8,12},{12,8},{16,20},{20,16},{24,28},{28,24},{1,5},{5... | collective-permute-start | bytes 61448 | tf_op jit(solution)/shard_map/ppermute | solution.py:335
  7.2 0.7 %copy-start.7 = (s32[128,6]{0,1:T(8,128)S(1)}, s32[128,6]{0,1:T(8,128)}, u32[]{:S(2)}) copy-start(s32[128,6]{0,1:T(8,128)} %param.13) | copy-start | bytes 9220
  7.2 0.7 %copy-start.9 = (f32[5]{0:T(128)S(1)}, f32[5]{0:T(128)}, u32[]{:S(2)}) copy-start(f32[5]{0:T(128)} %param.19) | copy-start | bytes 64
  9.5 5.0 %collective-permute-start.4 = (bf16[16,640]{1,0:T(8,128)(2,1)S(1)}, bf16[16,640]{1,0:T(8,128)(2,1)S(1)}, u32[]{:S(2)}, u32[]{:S(2)}) collective-permute-start(bf16[16,640]{1,0:T(8,128)(2,1)S(1)} %get-tuple-element.45), channel_id=1, source_target_pairs={{0,1},{1,0},{2,3},{3,2},{4,5},{5,4},{6,7},{7,6},{8,9},{9,8},{10,11... | collective-permute-start | bytes 61448 | tf_op jit(solution)/shard_map/ppermute | solution.py:362
  11.4 3.1 %collective-permute-start.5 = (bf16[16,640]{1,0:T(8,128)(2,1)S(1)}, bf16[16,640]{1,0:T(8,128)(2,1)S(1)}, u32[]{:S(2)}, u32[]{:S(2)}) collective-permute-start(bf16[16,640]{1,0:T(8,128)(2,1)S(1)} %get-tuple-element.46), channel_id=1, source_target_pairs={{1,2},{2,1},{5,6},{6,5},{9,10},{10,9},{13,14},{14,13},{17,18},{18,... | collective-permute-start | bytes 61448 | tf_op jit(solution)/shard_map/ppermute | solution.py:362
  11.4 3.8 %collective-permute-start.6 = (bf16[16,640]{1,0:T(8,128)(2,1)S(1)}, bf16[16,640]{1,0:T(8,128)(2,1)S(1)}, u32[]{:S(2)}, u32[]{:S(2)}) collective-permute-start(bf16[16,640]{1,0:T(8,128)(2,1)S(1)} %get-tuple-element.47), channel_id=1, source_target_pairs={{4,8},{8,4},{12,16},{16,12},{20,24},{24,20},{5,9},{9,5},{13,17},{1... | collective-permute-start | bytes 61448 | tf_op jit(solution)/shard_map/ppermute | solution.py:362
  12.4 2.8 %collective-permute-start.7 = (bf16[16,640]{1,0:T(8,128)(2,1)S(1)}, bf16[16,640]{1,0:T(8,128)(2,1)S(1)}, u32[]{:S(2)}, u32[]{:S(2)}) collective-permute-start(bf16[16,640]{1,0:T(8,128)(2,1)S(1)} %get-tuple-element.48), channel_id=1, source_target_pairs={{0,4},{4,0},{8,12},{12,8},{16,20},{20,16},{24,28},{28,24},{1,5},{5... | collective-permute-start | bytes 61448 | tf_op jit(solution)/shard_map/ppermute | solution.py:362

commit v3 on v2

--- a/solution.py
+++ b/solution.py
@@ -18,6 +18,7 @@
 FIELD = VARS * MODES
 POINTS = FACES * FACEPTS
 AXES = ("rx", "ry")
+LATER = (1, 2, 0, 3)
 F32 = jnp.float32
 BF16 = jnp.bfloat16
 VMEM_BYTES = 16 * 1024 * 1024
@@ -47,13 +48,13 @@
     for j in {0, ny - 1 if ny % 2 == 0 else 0}:
         for i in range(0, nx - 1, 2):
             y_odd += both(joint(i, j), joint(i + 1, j))
-    return y_even, y_odd, x_odd, x_even
+    return y_odd, y_even, x_odd, x_even
 
 
 def directions():
     odd_x = lax.rem(lax.axis_index("rx"), 2)
     odd_y = lax.rem(lax.axis_index("ry"), 2)
-    return 3 - odd_y, 2 + odd_y, odd_x, 1 - odd_x
+    return 2 + odd_y, 3 - odd_y, odd_x, 1 - odd_x
 
 
 def iota(shape, dim):
@@ -296,8 +297,9 @@
     part_ref[...] = total
 
 
-def last_kernel(part_ref, coef_ref, hot_ref, a_ref, b_ref, c_ref, d_ref, out_ref):
-    packed = jnp.concatenate([ref[...] for ref in (a_ref, b_ref, c_ref, d_ref)], axis=0)
+def last_kernel(part_ref, coef_ref, hot_ref, *refs):
+    out_ref = refs[4]
+    packed = jnp.concatenate([refs[LATER.index(j)][...] for j in range(4)], axis=0)
     terms = dot(packed, coef_ref[...]) * hot_ref[...].astype(F32)
     sums = jnp.sum(terms, axis=0, keepdims=True)
     total = jnp.sum(part_ref[...], axis=0, keepdims=True)
@@ -359,7 +361,7 @@
         moved=10**6,
     )(primal_t, adjoint_t, nbr, recon, deriv, lift, face_trace.T, pick, jacob.transpose(1, 0, 2), dissip[None])
     second = call(listed_kernel, [message] * 4)(listed, listed_hots, pair_recon, *got)
-    got_more = [lax.ppermute(m, AXES, pairs) for m, pairs in zip(second, perms)]
+    got_more = [lax.ppermute(second[j], AXES, perms[j]) for j in LATER]
     part, coef = call(
         middle_kernel,
         [shape((8, count), F32), shape((WIDE, 4 * count), BF16)],

time: 16.1 us -> 15.1 us (0.938)
  waiting for transfers between devices: 0.82 us -> 0.26 us
  starting transfers between devices: 9.32 us -> 8.78 us
    ppermute x4, starting transfers between devices: 3.34 us -> 2.6 us  [shards(): got_more = [lax.ppermute(second[j], AXES, perms[j]) for j in LATER]]
    ppermute x4, waiting for transfers between devices: 0.68 us -> 0.01 us  [shards(): got_more = [lax.ppermute(second[j], AXES, perms[j]) for j in LATER]]
    ppermute x4, starting transfers between devices: 5.98 us -> 6.18 us  [shards(): got = [lax.ppermute(m, AXES, pairs) for m, pairs in zip(first, perms)]]
  transfers between devices with their start and end apart: 8 -> 8, of which waited for: 2 -> 1; matrix products, arithmetic and copies ran while one was open for 0% -> 0% of each run, Pallas kernels for 17% -> 19%
where the time goes in v3:
time: 15.1 us; the launch traced here: 14.9 us
  starting transfers between devices  8.78 us (58%)
  Pallas kernels  4.12 us (27%)
  local copies, waits for them, and re-layouts  1.58 us (10%)
  waiting for transfers between devices  0.26 us (2%)
    ppermute x4, starting transfers between devices, shards(): got = [lax.ppermute(m, AXES, pairs) for m, pairs in zip(first, perms)]  6.18 us
    pallas_call x6, Pallas kernels, run(): pl.pallas_call(kernel, out_shape=outs, in_specs=[pl.BlockSpec(memory_spac...  4.12 us
    ppermute x4, starting transfers between devices, shards(): got_more = [lax.ppermute(second[j], AXES, perms[j]) for j in LATER]  2.6 us
    unnamed x20, local copies, waits for them, and re-layouts  1.58 us
  transfers between devices with their start and end apart: 8, of which 1 were waited for; matrix products, arithmetic and copies ran while one was open for 0% of the time, Pallas kernels for 19%

profile of v3, /device:TPU:0, one launch (start us, length us, event | category | flops | bytes accessed | tf_op | source)
XLA Modules:
  0.0 14.9 jit_solution(6045525007509065378)
XLA Ops:
  0.0 0.0 copy-start.8
  0.0 0.9 %copy-done.2 = bf16[128,320]{0,1:T(8,128)(2,1)S(1)} copy-done((bf16[128,320]{0,1:T(8,128)(2,1)S(1)}, bf16[128,320]{0,1:T(8,128)(2,1)}, u32[]{:S(2)}) %copy-start.2) | copy-done | bytes 81944
  0.9 0.0 copy-done.3
  0.9 0.0 copy-start.5
  1.0 0.3 %shard_map.101 = (bf16[64,128]{1,0:T(8,128)(2,1)S(1)}, bf16[16,640]{1,0:T(8,128)(2,1)S(1)}, bf16[16,640]{1,0:T(8,128)(2,1)S(1)}, bf16[16,640]{1,0:T(8,128)(2,1)S(1)}, bf16[16,640]{1,0:T(8,128)(2,1)S(1)}) custom-call(f32[64,16]{1,0:T(8,128)S(1)} %shard_map.100.mask_ref, bf16[320,128]{1,0:T(8,128)(2,1)S(1)} %bitcast.7, bf16[320,128]{1,0:T(8,128)(2,1)S(1)} %bitcast.9, ...), custom_call_target="tpu_custom_call" | custom-call | flops 1000000000 | bytes 100000 | tf_op jit(solution)/shard_map/pallas_call | solution.py:314
  1.2 0.5 %collective-permute-start = (bf16[16,640]{1,0:T(8,128)(2,1)S(1)}, bf16[16,640]{1,0:T(8,128)(2,1)S(1)}, u32[]{:S(2)}, u32[]{:S(2)}) collective-permute-start(bf16[16,640]{1,0:T(8,128)(2,1)S(1)} %get-tuple-element.36), channel_id=1, source_target_pairs={{1,2},{2,1},{5,6},{6,5},{9,10},{10,9},{13,14},{14,13},{17,18},{18,... | collective-permute-start | bytes 61448 | tf_op jit(solution)/shard_map/ppermute | solution.py:337
  1.7 4.0 %collective-permute-start.1 = (bf16[16,640]{1,0:T(8,128)(2,1)S(1)}, bf16[16,640]{1,0:T(8,128)(2,1)S(1)}, u32[]{:S(2)}, u32[]{:S(2)}) collective-permute-start(bf16[16,640]{1,0:T(8,128)(2,1)S(1)} %get-tuple-element.37), channel_id=1, source_target_pairs={{0,1},{1,0},{2,3},{3,2},{4,5},{5,4},{6,7},{7,6},{8,9},{9,8},{10,11... | collective-permute-start | bytes 61448 | tf_op jit(solution)/shard_map/ppermute | solution.py:337
  5.7 0.0 collective-permute-start.2
  5.7 1.7 %collective-permute-start.3 = (bf16[16,640]{1,0:T(8,128)(2,1)S(1)}, bf16[16,640]{1,0:T(8,128)(2,1)S(1)}, u32[]{:S(2)}, u32[]{:S(2)}) collective-permute-start(bf16[16,640]{1,0:T(8,128)(2,1)S(1)} %get-tuple-element.39), channel_id=1, source_target_pairs={{0,4},{4,0},{8,12},{12,8},{16,20},{20,16},{24,28},{28,24},{1,5},{5... | collective-permute-start | bytes 61448 | tf_op jit(solution)/shard_map/ppermute | solution.py:337
  7.4 0.6 %copy-done.7 = s32[128,6]{0,1:T(8,128)S(1)} copy-done((s32[128,6]{0,1:T(8,128)S(1)}, s32[128,6]{0,1:T(8,128)}, u32[]{:S(2)}) %copy-start.7) | copy-done | bytes 3096
  8.1 1.1 %shard_map.102 = (f32[128,1280]{1,0:T(8,128)S(1)}, f32[64,640]{1,0:T(8,128)S(1)}, bf16[64,512]{1,0:T(8,128)(2,1)S(1)}, bf16[256,64]{1,0:T(8,128)(2,1)S(1)}, bf16...) custom-call(bf16[320,128]{1,0:T(8,128)(2,1)S(1)} %bitcast.8, ...), custom_call_target="tpu_custom_call" | custom-call | flops 3000000000 | bytes 1000000 | tf_op jit(solution)/shard_map/pallas_call | solution.py:314
  9.2 0.0 collective-permute-done.a_ref
  9.2 0.0 collective-permute-done.1.b_ref
  9.2 0.2 %collective-permute-done.2.c_ref = bf16[16,640]{1,0:T(8,128)(2,1)S(1)} collective-permute-done((bf16[16,640]{1,0:T(8,128)(2,1)S(1)}, bf16[16,640]{1,0:T(8,128)(2,1)S(1)}, u32[]{:S(2)}, u32[]{:S(2)}) %collective-permute-start.2) | collective-permute-done | bytes 20512 | tf_op jit(solution)/shard_map/ppermute | solution.py:337
  9.5 0.0 collective-permute-done.3.d_ref
  9.5 0.3 %shard_map.104 = (bf16[16,640]{1,0:T(8,128)(2,1)S(1)}, bf16[16,640]{1,0:T(8,128)(2,1)S(1)}, bf16[16,640]{1,0:T(8,128)(2,1)S(1)}, bf16[16,640]{1,0:T(8,128)(2,1)S(1)}) custom-call(f32[64,640]{1,0:T(8,128)S(1)} %get-tuple-element.42.near_ref, bf16[256,64]{1,0:T(8,128)(2,1)S(1)} %get-tuple-element.43.hot_ref, bf16[512,256]{1,0:T(8,128)(2,1)S(1)} %get-tuple-element.44.recon_ref, ...), custom_call_target="tpu_custom_call" | custom-call | flops 1000000 | bytes 100000 | tf_op jit(solution)/shard_map/pallas_call | solution.py:314
  9.8 0.3 %collective-permute-start.4 = (bf16[16,640]{1,0:T(8,128)(2,1)S(1)}, bf16[16,640]{1,0:T(8,128)(2,1)S(1)}, u32[]{:S(2)}, u32[]{:S(2)}) collective-permute-start(bf16[16,640]{1,0:T(8,128)(2,1)S(1)} %get-tuple-element.45), channel_id=1, source_target_pairs={{0,1},{1,0},{2,3},{3,2},{4,5},{5,4},{6,7},{7,6},{8,9},{9,8},{10,11... | collective-permute-start | bytes 61448 | tf_op jit(solution)/shard_map/ppermute | solution.py:364
  10.1 1.8 %collective-permute-start.5 = (bf16[16,640]{1,0:T(8,128)(2,1)S(1)}, bf16[16,640]{1,0:T(8,128)(2,1)S(1)}, u32[]{:S(2)}, u32[]{:S(2)}) collective-permute-start(bf16[16,640]{1,0:T(8,128)(2,1)S(1)} %get-tuple-element.46), channel_id=1, source_target_pairs={{4,8},{8,4},{12,16},{16,12},{20,24},{24,20},{5,9},{9,5},{13,17},{1... | collective-permute-start | bytes 61448 | tf_op jit(solution)/shard_map/ppermute | solution.py:364
  11.9 0.0 collective-permute-start.6
  11.9 0.5 %collective-permute-start.7 = (bf16[16,640]{1,0:T(8,128)(2,1)S(1)}, bf16[16,640]{1,0:T(8,128)(2,1)S(1)}, u32[]{:S(2)}, u32[]{:S(2)}) collective-permute-start(bf16[16,640]{1,0:T(8,128)(2,1)S(1)} %get-tuple-element.48), channel_id=1, source_target_pairs={{0,4},{4,0},{8,12},{12,8},{16,20},{20,16},{24,28},{28,24},{1,5},{5... | collective-permute-start | bytes 61448 | tf_op jit(solution)/shard_map/ppermute | solution.py:364
  12.4 1.6 %shard_map.103 = (f32[8,128]{1,0:T(8,128)S(1)}, bf16[640,512]{1,0:T(8,128)(2,1)S(1)}) custom-call(f32[128,1280]{1,0:T(8,128)S(1)} %get-tuple-element.28.near_ref, bf16[64,512]{1,0:T(8,128)(2,1)S(1)} %get-tuple-element.29.hot_ref, bf16[128,256]{1,0:T(8,128)(2,1)S(1)} %get-tuple-element.30.recon_ref, bf16[128,768]{1,0:T(8,128)(2,1)S(1)} %get-tuple-element.31.local_ref, ...), custom_call_target="tpu_custom_call" | custom-call | flops 1000000000 | bytes 1000000 | tf_op jit(solution)/shard_map/pallas_call | solution.py:314
  14.1 0.0 collective-permute-done.6.refs_2_
  14.1 0.0 collective-permute-done.7.refs_3_
  14.1 0.8 %shard_map.105 = f32[1,128]{1,0:T(1,128)} custom-call(f32[8,128]{1,0:T(8,128)S(1)} %get-tuple-element.40.part_ref, bf16[640,512]{1,0:T(8,128)(2,1)S(1)} %get-tuple-element.41.coef_ref, bf16[64,512]{1,0:T(8,128)(2,1)S(1)} %get-tuple-element.29.hot_ref, bf16[16,640]{1,0:T(8,128)(2,1)S(1)} %collective-permute-done.4.refs_0_, ...), custom_call_target="tpu_custom_call" | custom-call | flops 1000000 | bytes 100000 | tf_op jit(solution)/shard_map/pallas_call | solution.py:314
  (18 shorter events, 0.0 us)
Async XLA Ops:
  0.0 0.9 %copy-start.2 = (bf16[128,320]{0,1:T(8,128)(2,1)S(1)}, bf16[128,320]{0,1:T(8,128)(2,1)}, u32[]{:S(2)}) copy-start(bf16[128,320]{0,1:T(8,128)(2,1)} %param.10) | copy-start | bytes 245764
  0.0 0.9 %copy-start.3 = (bf16[128,320]{0,1:T(8,128)(2,1)S(1)}, bf16[128,320]{0,1:T(8,128)(2,1)}, u32[]{:S(2)}) copy-start(bf16[128,320]{0,1:T(8,128)(2,1)} %param.11) | copy-start | bytes 245764
  0.0 0.9 %copy-start.8 = (s32[4,16]{1,0:T(4,128)S(1)}, s32[4,16]{1,0:T(4,128)}, u32[]{:S(2)}) copy-start(s32[4,16]{1,0:T(4,128)} %send_ref.1) | copy-start | bytes 772
  0.9 6.5 %copy-start = (bf16[7,64,125]{2,1,0:T(8,128)(2,1)S(1)}, bf16[7,64,125]{2,1,0:T(8,128)(2,1)}, u32[]{:S(2)}) copy-start(bf16[7,64,125]{2,1,0:T(8,128)(2,1)} %recon_ref.1) | copy-start | bytes 336004
  0.9 6.5 %copy-start.1 = (bf16[3,125,125]{2,1,0:T(8,128)(2,1)S(1)}, bf16[3,125,125]{2,1,0:T(8,128)(2,1)}, u32[]{:S(2)}) copy-start(bf16[3,125,125]{2,1,0:T(8,128)(2,1)} %deriv_ref.1) | copy-start | bytes 281254
  0.9 6.5 %copy-start.4 = (bf16[150,125]{1,0:T(8,128)(2,1)S(1)}, bf16[150,125]{1,0:T(8,128)(2,1)}, u32[]{:S(2)}) copy-start(bf16[150,125]{1,0:T(8,128)(2,1)} %lift_ref.1) | copy-start | bytes 112504
  0.9 6.5 %copy-start.5 = (bf16[125,150]{0,1:T(8,128)(2,1)S(1)}, bf16[125,150]{0,1:T(8,128)(2,1)}, u32[]{:S(2)}) copy-start(bf16[125,150]{0,1:T(8,128)(2,1)} %param.17) | copy-start | bytes 112504
  1.2 6.2 %copy-start.6 = (f32[3,5,5]{2,0,1:T(4,128)S(1)}, f32[3,5,5]{2,0,1:T(4,128)}, u32[]{:S(2)}) copy-start(f32[3,5,5]{2,0,1:T(4,128)} %param.16) | copy-start | bytes 904
  1.2 8.0 %collective-permute-start = (bf16[16,640]{1,0:T(8,128)(2,1)S(1)}, bf16[16,640]{1,0:T(8,128)(2,1)S(1)}, u32[]{:S(2)}, u32[]{:S(2)}) collective-permute-start(bf16[16,640]{1,0:T(8,128)(2,1)S(1)} %get-tuple-element.36), channel_id=1, source_target_pairs={{1,2},{2,1},{5,6},{6,5},{9,10},{10,9},{13,14},{14,13},{17,18},{18,... | collective-permute-start | bytes 61448 | tf_op jit(solution)/shard_map/ppermute | solution.py:337
  1.7 7.5 %collective-permute-start.1 = (bf16[16,640]{1,0:T(8,128)(2,1)S(1)}, bf16[16,640]{1,0:T(8,128)(2,1)S(1)}, u32[]{:S(2)}, u32[]{:S(2)}) collective-permute-start(bf16[16,640]{1,0:T(8,128)(2,1)S(1)} %get-tuple-element.37), channel_id=1, source_target_pairs={{0,1},{1,0},{2,3},{3,2},{4,5},{5,4},{6,7},{7,6},{8,9},{9,8},{10,11... | collective-permute-start | bytes 61448 | tf_op jit(solution)/shard_map/ppermute | solution.py:337
  5.7 3.8 %collective-permute-start.2 = (bf16[16,640]{1,0:T(8,128)(2,1)S(1)}, bf16[16,640]{1,0:T(8,128)(2,1)S(1)}, u32[]{:S(2)}, u32[]{:S(2)}) collective-permute-start(bf16[16,640]{1,0:T(8,128)(2,1)S(1)} %get-tuple-element.38), channel_id=1, source_target_pairs={{4,8},{8,4},{12,16},{16,12},{20,24},{24,20},{5,9},{9,5},{13,17},{1... | collective-permute-start | bytes 61448 | tf_op jit(solution)/shard_map/ppermute | solution.py:337
  5.7 3.8 %collective-permute-start.3 = (bf16[16,640]{1,0:T(8,128)(2,1)S(1)}, bf16[16,640]{1,0:T(8,128)(2,1)S(1)}, u32[]{:S(2)}, u32[]{:S(2)}) collective-permute-start(bf16[16,640]{1,0:T(8,128)(2,1)S(1)} %get-tuple-element.39), channel_id=1, source_target_pairs={{0,4},{4,0},{8,12},{12,8},{16,20},{20,16},{24,28},{28,24},{1,5},{5... | collective-permute-start | bytes 61448 | tf_op jit(solution)/shard_map/ppermute | solution.py:337
  7.4 0.7 %copy-start.7 = (s32[128,6]{0,1:T(8,128)S(1)}, s32[128,6]{0,1:T(8,128)}, u32[]{:S(2)}) copy-start(s32[128,6]{0,1:T(8,128)} %param.13) | copy-start | bytes 9220
  7.4 0.7 %copy-start.9 = (f32[5]{0:T(128)S(1)}, f32[5]{0:T(128)}, u32[]{:S(2)}) copy-start(f32[5]{0:T(128)} %param.19) | copy-start | bytes 64
  9.8 4.2 %collective-permute-start.4 = (bf16[16,640]{1,0:T(8,128)(2,1)S(1)}, bf16[16,640]{1,0:T(8,128)(2,1)S(1)}, u32[]{:S(2)}, u32[]{:S(2)}) collective-permute-start(bf16[16,640]{1,0:T(8,128)(2,1)S(1)} %get-tuple-element.45), channel_id=1, source_target_pairs={{0,1},{1,0},{2,3},{3,2},{4,5},{5,4},{6,7},{7,6},{8,9},{9,8},{10,11... | collective-permute-start | bytes 61448 | tf_op jit(solution)/shard_map/ppermute | solution.py:364
  10.1 3.9 %collective-permute-start.5 = (bf16[16,640]{1,0:T(8,128)(2,1)S(1)}, bf16[16,640]{1,0:T(8,128)(2,1)S(1)}, u32[]{:S(2)}, u32[]{:S(2)}) collective-permute-start(bf16[16,640]{1,0:T(8,128)(2,1)S(1)} %get-tuple-element.46), channel_id=1, source_target_pairs={{4,8},{8,4},{12,16},{16,12},{20,24},{24,20},{5,9},{9,5},{13,17},{1... | collective-permute-start | bytes 61448 | tf_op jit(solution)/shard_map/ppermute | solution.py:364
  11.9 2.2 %collective-permute-start.6 = (bf16[16,640]{1,0:T(8,128)(2,1)S(1)}, bf16[16,640]{1,0:T(8,128)(2,1)S(1)}, u32[]{:S(2)}, u32[]{:S(2)}) collective-permute-start(bf16[16,640]{1,0:T(8,128)(2,1)S(1)} %get-tuple-element.47), channel_id=1, source_target_pairs={{1,2},{2,1},{5,6},{6,5},{9,10},{10,9},{13,14},{14,13},{17,18},{18,... | collective-permute-start | bytes 61448 | tf_op jit(solution)/shard_map/ppermute | solution.py:364
  11.9 2.2 %collective-permute-start.7 = (bf16[16,640]{1,0:T(8,128)(2,1)S(1)}, bf16[16,640]{1,0:T(8,128)(2,1)S(1)}, u32[]{:S(2)}, u32[]{:S(2)}) collective-permute-start(bf16[16,640]{1,0:T(8,128)(2,1)S(1)} %get-tuple-element.48), channel_id=1, source_target_pairs={{0,4},{4,0},{8,12},{12,8},{16,20},{20,16},{24,28},{28,24},{1,5},{5... | collective-permute-start | bytes 61448 | tf_op jit(solution)/shard_map/ppermute | solution.py:364
